TPU v7x, 32 devices: a whole 2x2x4 slice. The times are simulated.
32 devices in a mesh: rep: 4 (over x, core), dp: 8 (over z, y).
Axes of the slice: x: 2, y: 2, z: 4, core: 2. Of those that a mesh axis runs over, the one named last changes fastest.
Arguments:
- image_features: bfloat16 [4096, 1408], P(('rep', 'dp')), parts along dimension 0, may hold values from -24 to 24
- text_embed: bfloat16 [4096, 512], P(('rep', 'dp')), parts along dimension 0, may hold values from -24 to 24
- image_head: bfloat16 [5632, 512], P(('rep', 'dp')), parts along dimension 0, may hold values from -1 to 3
- logit_scale: float32 [1], replicated, may hold values from 10 to 40
Outputs:
- image_features_grad: bfloat16 [4096, 1408], P(('rep', 'dp')), parts along dimension 0
- text_embed_grad: bfloat16 [4096, 512], P(('rep', 'dp')), parts along dimension 0
- image_head_grad: float32 [5632, 512], P(('rep', 'dp')), parts along dimension 0
There are 4 independent parts, one for each index of `rep`. A program takes and returns all parts, laid end to end along the dimension named above; an argument that names none is the same for every part. Nothing has to cross between parts.
All inputs are finite; a program needn't handle non-finite values.
Results may differ from a plain program's by a relative error of at most 0.02.
Values may be sent and summed in bfloat16 or wider, within the bound.
A program may use at most 64 MiB of HBM per device.

v0:
```python
import jax
import jax.numpy as jnp
from jax import lax
from jax.sharding import PartitionSpec as P


def unit_rows(embedding):
    inv_norm = lax.rsqrt(jnp.sum(embedding * embedding, axis=1, keepdims=True) + 1e-06)
    return (embedding * inv_norm, inv_norm)


def norm_backward(embedding, inv_norm, upstream):
    inner = jnp.sum(embedding * upstream, axis=1, keepdims=True)
    return (inv_norm * upstream - embedding * (inv_norm * inv_norm * inv_norm) * inner).astype(
        jnp.bfloat16
    )


def tile_logits(logit_mult, left_rows, right_rows):
    product = lax.dot_general(
        left_rows, right_rows, (((1,), (1,)), ((), ())), preferred_element_type=jnp.float32
    )
    return logit_mult * product


def pair_coef(logits, left_lse, right_lse, left_ids, right_ids):
    label = (left_ids[:, None] == right_ids[None, :]).astype(jnp.float32)
    values = (
        jnp.exp(logits - left_lse[:, None]) + jnp.exp(logits - right_lse[None, :]) - 2.0 * label
    )
    return values.astype(jnp.bfloat16)


def local(image_features, text_embed, image_head, logit_scale):
    logit_mult = logit_scale[0]
    row_count = image_features.shape[0]
    own_ids = lax.axis_index("dp") * row_count + jnp.arange(row_count, dtype=jnp.int32)
    head_full = lax.all_gather(image_head, "dp", axis=0, tiled=True)
    img_emb = jnp.dot(image_features, head_full, preferred_element_type=jnp.float32)
    img_scaled, img_inv = unit_rows(img_emb)
    img_unit = img_scaled.astype(jnp.bfloat16)
    txt_emb = text_embed.astype(jnp.float32)
    txt_scaled, txt_inv = unit_rows(txt_emb)
    txt_unit = txt_scaled.astype(jnp.bfloat16)
    exp_tile = jnp.exp(
        tile_logits(logit_mult, img_unit, lax.all_gather(txt_unit, "dp", axis=0, tiled=True))
    )
    col_part = jnp.sum(exp_tile, axis=0)
    row_sum, col_part = (jnp.sum(exp_tile, axis=1), col_part)
    row_lse = jnp.log(row_sum)
    col_lse = jnp.log(lax.psum_scatter(col_part, "dp", scatter_dimension=0, tiled=True))
    row_all, col_all = (
        lax.all_gather(row_lse, "dp", axis=0, tiled=True),
        lax.all_gather(col_lse, "dp", axis=0, tiled=True),
    )
    img_piece = lax.all_gather(img_unit, "dp", axis=0, tiled=True)
    txt_piece = lax.all_gather(txt_unit, "dp", axis=0, tiled=True)
    count = img_piece.shape[0]
    piece_ids = jnp.arange(count, dtype=jnp.int32)
    img_coef = pair_coef(
        tile_logits(logit_mult, img_unit, txt_piece), row_lse, col_all, own_ids, piece_ids
    )
    txt_coef = pair_coef(
        tile_logits(logit_mult, txt_unit, img_piece), col_lse, row_all, own_ids, piece_ids
    )
    img_acc = jnp.dot(img_coef, txt_piece, preferred_element_type=jnp.float32)
    txt_acc = jnp.dot(txt_coef, img_piece, preferred_element_type=jnp.float32)
    img_unit_grad = logit_mult * img_acc
    txt_unit_grad = logit_mult * txt_acc
    img_emb_grad = norm_backward(img_emb, img_inv, img_unit_grad)
    text_embed_grad = norm_backward(txt_emb, txt_inv, txt_unit_grad)
    image_features_grad = lax.dot_general(
        img_emb_grad, head_full, (((1,), (1,)), ((), ())), preferred_element_type=jnp.float32
    ).astype(jnp.bfloat16)
    head_partial = lax.dot_general(
        image_features, img_emb_grad, (((0,), (0,)), ((), ())), preferred_element_type=jnp.float32
    )
    image_head_grad = lax.psum_scatter(
        head_partial.astype(jnp.bfloat16), "dp", scatter_dimension=0, tiled=True
    ).astype(jnp.float32)
    return (image_features_grad, text_embed_grad, image_head_grad)


def solution(mesh):
    in_specs = (P(("rep", "dp"), None), P(("rep", "dp"), None), P(("rep", "dp"), None), P())
    out_specs = (P(("rep", "dp"), None), P(("rep", "dp"), None), P(("rep", "dp"), None))
    return jax.shard_map(local, mesh=mesh, in_specs=in_specs, out_specs=out_specs, check_vma=False)
```

profile of v0, /device:TPU:0, one launch (start us, length us, event | category | flops | bytes accessed | tf_op | source)
XLA Modules:
  0.0 214.3 jit_solution(13222421687849722253)
XLA Ops:
  7.2 0.0 copy-start
  7.2 0.0 all-gather.6.cloned.1.call-start
  7.2 0.7 all-gather.6.cloned.1.call-update
  7.9 0.0 all-gather.8.cloned.1.call-start
  8.0 1.0 fusion.3
  9.0 1.7 fusion.4
  10.6 0.0 copy-start.4
  10.6 0.0 all-gather.8.cloned.1.call-update
  10.7 0.0 all-gather.10.cloned.1.call-start
  10.7 45.3 %all-gather.6.cloned.1.call-done = bf16[1408,512]{1,0:T(8,128)(2,1)} async-done(((bf16[176,512]{1,0:T(8,128)(2,1)}), bf16[1408,512]{1,0:T(8,128)(2,1)}) %all-gather.6.cloned.1.call-update) | async-done | bytes 1441808 | tf_op jit(solution)/shard_map/all_gather | solution.py:38
  56.0 0.0 copy-done
  56.0 1.8 multiply_reduce_fusion.1
  57.8 0.8 multiply_convert_fusion
  58.6 0.0 all-gather.10.cloned.1.call-update
  58.6 0.0 reduce-scatter.4.cloned.1.call-start
  59.3 0.0 copy-done.4
  59.3 0.6 dynamic-slice
  60.6 36.6 %all-gather.8.cloned.1.call-done = bf16[1024,512]{1,0:T(8,128)(2,1)} async-done(((bf16[128,512]{1,0:T(8,128)(2,1)}), bf16[1024,512]{1,0:T(8,128)(2,1)}) %all-gather.8.cloned.1.call-update) | async-done | bytes 1048592 | tf_op jit(solution)/shard_map/all_gather | solution.py:57
  97.2 0.0 copy-start.3
  97.2 1.9 exponential_reduce_fusion.1
  99.2 19.3 %all-reduce = f32[1024]{0:T(1024)S(1)} all-reduce(f32[1024]{0:T(1024)S(1)} %get-tuple-element.10), channel_id=2, replica_groups=mesh['rep'=4,'dp'=8] {'dp'}, use_global_device_ids=true, to_apply=%region_4.0.clone | all-reduce | flops 1024 | bytes 8192
  118.5 0.1 fusion.38
  118.5 16.2 %all-gather = f32[8,1,128]{2,1,0:T(1,128)S(1)} all-gather(f32[1,1,128]{2,1,0:T(1,128)S(1)} %fusion.38), channel_id=1, replica_groups=mesh['rep'=4,'dp'=8] {'dp'}, dimensions={0}, use_global_device_ids=true | all-gather | bytes 4608 | tf_op jit(solution)/shard_map/all_gather | solution.py:54
  134.7 0.0 copy-done.3
  134.7 0.5 multiply_reduce_fusion
  135.2 0.1 subtract_convert_fusion
  135.3 0.6 fusion
  135.9 1.6 copy.9
  137.5 0.0 copy-start.1
  137.5 0.0 copy-start.2
  137.5 0.0 reduce-scatter.4.cloned.1.call-update
  137.5 18.3 %all-gather.1 = f32[8,1,128]{2,1,0:T(1,128)S(1)} all-gather(f32[1,1,128]{2,1,0:T(1,128)S(1)} %get-tuple-element.13), channel_id=1, replica_groups=mesh['rep'=4,'dp'=8] {'dp'}, dimensions={0}, use_global_device_ids=true | all-gather | bytes 4608 | tf_op jit(solution)/shard_map/all_gather | solution.py:53
  155.8 0.1 dynamic-slice_log_fusion
  155.9 0.0 copy-done.1
  155.9 1.4 convolution_convert_fusion.1
  157.3 0.0 all-gather.10.cloned.1.call-done
  157.3 0.0 copy-done.2
  157.3 2.4 %fusion.8 = (f32[128]{0:T(128)S(1)}, f32[128,512]{1,0:T(8,128)S(1)}) fusion(bf16[128,512]{1,0:T(8,128)(2,1)S(1)} %copy-done.2, bf16[1024,512]{1,0:T(8,128)(2,1)} %all-gather.10.cloned.1.call-done, f32[1024]{0:T(1024)S(1)} %bitcast.25, f32[128]{0:T(128)S(1)} %dynamic-slice_log_fusion, s32[128]{0:T(128)S(1)} %iota_add_fusion, f32[]{:T(128)} %bitcast.24, ...), kind=kOutput, calls=%fused_computation.23 | convolution fusion | flops 269942656 | bytes 1447940 | tf_op jit(solution)/shard_map/dot_general | solution.py:67
  159.6 0.8 fusion.7
  160.4 45.4 %reduce-scatter.4.cloned.1.call-done = bf16[176,512]{1,0:T(8,128)(2,1)} async-done(((bf16[1408,512]{1,0:T(8,128)(2,1)}), bf16[176,512]{1,0:T(8,128)(2,1)}) %reduce-scatter.4.cloned.1.call-update) | async-done | bytes 180240
  205.9 1.1 copy.10
  206.9 0.9 copy.8
  (4 shorter events, 0.0 us)
Async XLA Ops:
  7.2 48.8 %copy-start = (bf16[128,1408]{1,0:T(8,128)(2,1)S(1)}, bf16[128,1408]{1,0:T(8,128)(2,1)}, u32[]{:S(2)}) copy-start(bf16[128,1408]{1,0:T(8,128)(2,1)} %param.4) | copy-start | bytes 1081348
  7.2 48.8 %all-gather.6.cloned.1.call-start = ((), (), s32[]{:S(2)}) async-start(), calls=%async_computation.1 | async-start | bytes 1622016 | tf_op jit(solution)/shard_map/all_gather | solution.py:38
  7.9 89.3 %all-gather.8.cloned.1.call-start = ((), (), s32[]{:S(2)}) async-start(), calls=%async_computation.2 | async-start | bytes 1179648 | tf_op jit(solution)/shard_map/all_gather | solution.py:57
  10.6 48.7 %copy-start.4 = (u32[32]{0:T(128)S(1)}, u32[32]{0:T(128)}, u32[]{:S(2)}) copy-start(u32[32]{0:T(128)} %constant.16) | copy-start | bytes 388
  10.7 146.6 %all-gather.10.cloned.1.call-start = ((), (), s32[]{:S(2)}) async-start(), calls=%async_computation.3 | async-start | bytes 1179648 | tf_op jit(solution)/shard_map/all_gather | solution.py:56
  58.6 147.3 %reduce-scatter.4.cloned.1.call-start = ((), (), s32[]{:S(2)}) async-start(), calls=%async_computation.4 | async-start | bytes 1622016
  97.2 37.5 %copy-start.3 = (bf16[1024,512]{1,0:T(8,128)(2,1)S(1)}, bf16[1024,512]{1,0:T(8,128)(2,1)}, u32[]{:S(2)}) copy-start(bf16[1024,512]{1,0:T(8,128)(2,1)} %all-gather.8.cloned.1.call-done) | copy-start | bytes 3145732
  137.5 18.4 %copy-start.1 = (bf16[1408,512]{1,0:T(8,128)(2,1)S(1)}, bf16[1408,512]{1,0:T(8,128)(2,1)}, u32[]{:S(2)}) copy-start(bf16[1408,512]{1,0:T(8,128)(2,1)} %all-gather.6.cloned.1.call-done) | copy-start | bytes 4325380
  137.5 19.8 %copy-start.2 = (bf16[128,512]{1,0:T(8,128)(2,1)S(1)}, bf16[128,512]{1,0:T(8,128)(2,1)}, u32[]{:S(2)}) copy-start(bf16[128,512]{1,0:T(8,128)(2,1)} %param.5) | copy-start | bytes 393220
Sparse Core Ops, SparseCore 0:
  10.2 45.7 all-gather.5
  58.7 38.4 all-gather.7
  99.9 38.9 all-gather.9
  142.2 63.6 reduce-scatter.3
where the time goes:
time: 215 us; the launch traced here: 214 us
  waiting for transfers between devices  128 us (60%)
  blocking collectives  53.8 us (25%)
  between operations  15.1 us (7%)
  matrix products  8.53 us (4%)
  other arithmetic  4.36 us (2%)
  local copies, waits for them, and re-layouts  4.29 us (2%)
    unnamed x5, waiting for transfers between devices  46.2 us
    all_gather x1, waiting for transfers between devices, local(): head_full = lax.all_gather(image_head, 'dp', axis=0, tiled=True)  45.3 us
    all_gather x1, waiting for transfers between devices, local(): txt_piece = lax.all_gather(txt_unit, 'dp', axis=0, tiled=True)  36.6 us
    unnamed x1, blocking collectives  19.3 us
    all_gather x1, blocking collectives, local(): lax.all_gather(row_lse, 'dp', axis=0, tiled=True)  18.3 us
    all_gather x1, blocking collectives, local(): lax.all_gather(col_lse, 'dp', axis=0, tiled=True)  16.2 us
  transfers between devices with their start and end apart: 4, of which 3 were waited for; matrix products, arithmetic and copies ran while one was open for 7% of the time, Pallas kernels for 0%

commit v1 on v0

--- a/solution.py
+++ b/solution.py
@@ -1,6 +1,10 @@
+import functools
+
 import jax
 import jax.numpy as jnp
 from jax import lax
+from jax.experimental import pallas as pl
+from jax.experimental.pallas import tpu as pltpu
 from jax.sharding import PartitionSpec as P
 
 
@@ -81,7 +85,297 @@
     return (image_features_grad, text_embed_grad, image_head_grad)
 
 
+MESH = pl.DeviceIdType.MESH
+HEAD, TEXT, IMAGE, GRAD = range(4)
+ROWS_ROWS = (((1,), (1,)), ((), ()))
+COLS_COLS = (((0,), (0,)), ((), ()))
+
+
+def place_of(index, n):
+    depth, side = lax.div(index, 2), lax.rem(index, 2)
+    return depth + side * (n - 1 - 2 * depth)
+
+
+def index_at(place, n):
+    place = lax.rem(place + 2 * n, n)
+    side = lax.div(place, n // 2)
+    return 2 * (place + side * (n - 1 - 2 * place)) + side
+
+
+def step_kernel(
+    n,
+    feat_ref,
+    text_ref,
+    head_ref,
+    scale_ref,
+    feat_grad_ref,
+    text_grad_ref,
+    head_grad_ref,
+    head_all,
+    text_all,
+    image_all,
+    feat_blocks,
+    feat_t_blocks,
+    exp_all,
+    inv_rows,
+    inv_cols,
+    outgoing,
+    incoming,
+    send_sem,
+    recv_sem,
+):
+    rows, width = text_ref.shape
+    depth = head_ref.shape[0]
+    half = width // 2
+    messages = n - 1
+    me = lax.axis_index("dp")
+    place = place_of(me, n)
+    partner = {+1: index_at(place + 1, n), -1: index_at(place - 1, n)}
+
+    barrier = pltpu.get_barrier_semaphore()
+    for way in (1, -1):
+        pl.semaphore_signal(barrier, inc=1, device_id={"dp": partner[way]}, device_id_type=MESH)
+
+    head_all[pl.ds(pl.multiple_of(me * depth, 16), depth), :] = head_ref[...]
+    pl.semaphore_wait(barrier, 2)
+
+    def columns(way, m):
+        first = (m % 2 == 0) == (way == 1)
+        return pl.ds(0 if first else half, half)
+
+    def remote(kind, way, m, src, dst):
+        side = 0 if way == 1 else 1
+        return pltpu.make_async_remote_copy(
+            src_ref=src,
+            dst_ref=dst,
+            send_sem=send_sem.at[kind, side, m],
+            recv_sem=recv_sem.at[kind, side, m],
+            device_id={"dp": partner[way]},
+            device_id_type=MESH,
+        )
+
+    gathered = {HEAD: (head_all, depth), TEXT: (text_all, rows), IMAGE: (image_all, rows)}
+
+    def gather_copy(kind, way, m, origin_shift):
+        buf, block = gathered[kind]
+        owner = index_at(place - way * origin_shift, n)
+        ref = buf.at[pl.ds(pl.multiple_of(owner * block, 16), block), columns(way, m)]
+        return remote(kind, way, m, ref, ref)
+
+    def gather_send(kind, m):
+        for way in (1, -1):
+            if m >= 2:
+                gather_copy(kind, way, m - 2, m // 2).wait_recv()
+            gather_copy(kind, way, m, m // 2).start()
+
+    def gather_last(kind):
+        for m in range(max(messages - 2, 0), messages):
+            for way in (1, -1):
+                gather_copy(kind, way, m, m // 2 + 1).wait_recv()
+
+    gather_send(HEAD, 0)
+    gather_send(HEAD, 1)
+
+    txt_emb = text_ref[...].astype(jnp.float32)
+    txt_scaled, txt_inv = unit_rows(txt_emb)
+    text_all[pl.ds(pl.multiple_of(me * rows, 16), rows), :] = txt_scaled.astype(jnp.bfloat16)
+    feat_t = feat_ref[...].astype(jnp.float32).T
+    for b in range(n):
+        block = feat_t[b * depth : (b + 1) * depth]
+        feat_t_blocks[b] = block.astype(jnp.bfloat16)
+        feat_blocks[b] = block.T.astype(jnp.bfloat16)
+
+    def emb_part(owner):
+        return jnp.dot(
+            feat_blocks[owner],
+            head_all[pl.ds(pl.multiple_of(owner * depth, 16), depth), :],
+            preferred_element_type=jnp.float32,
+        )
+
+    img_emb = emb_part(me)
+    for m in range(2, messages):
+        gather_send(HEAD, m)
+        if m % 2 == 1:
+            for way in (1, -1):
+                img_emb += emb_part(index_at(place - way * (m // 2), n))
+    gather_send(TEXT, 0)
+    gather_send(TEXT, 1)
+    gather_last(HEAD)
+    for way in (1, -1):
+        img_emb += emb_part(index_at(place - way * (n // 2 - 1), n))
+    img_emb += emb_part(index_at(place + n // 2, n))
+    img_scaled, img_inv = unit_rows(img_emb)
+    image_all[pl.ds(pl.multiple_of(me * rows, 16), rows), :] = img_scaled.astype(jnp.bfloat16)
+
+    for m in range(messages - 2):
+        gather_send(IMAGE, m)
+        gather_send(TEXT, m + 2)
+    gather_last(TEXT)
+
+    scale = scale_ref[0]
+
+    def exp_block(owner, col_sum):
+        at = pl.ds(pl.multiple_of(owner * rows, 16), rows)
+        values = jnp.exp(
+            scale
+            * lax.dot_general(
+                image_all[at, :], text_all[...], ROWS_ROWS, preferred_element_type=jnp.float32
+            )
+        )
+        exp_all[at, :] = values
+        inv_rows[at, :] = 1.0 / jnp.sum(values, axis=1, keepdims=True)
+        return col_sum + jnp.sum(values, axis=0, keepdims=True)
+
+    col_sum = exp_block(me, jnp.zeros((1, n * rows), jnp.float32))
+    for shift in range(1, n // 2):
+        m = messages - 2 + (shift - 1)
+        if m < messages:
+            gather_send(IMAGE, m)
+        if shift == n // 2 - 1:
+            gather_last(IMAGE)
+        for way in (1, -1):
+            col_sum = exp_block(index_at(place - way * shift, n), col_sum)
+    col_sum = exp_block(index_at(place + n // 2, n), col_sum)
+    inv_col = 1.0 / col_sum
+    inv_cols[...] = inv_col
+
+    own = pl.ds(pl.multiple_of(me * rows, 128), rows)
+    pairs = n * rows
+    row_ids = lax.broadcasted_iota(jnp.int32, (rows, pairs), 0) + me * rows
+    label = (row_ids == lax.broadcasted_iota(jnp.int32, (rows, pairs), 1)).astype(jnp.float32)
+    img_coef = exp_all[own, :] * (inv_rows[own, :] + inv_col) - 2.0 * label
+    img_acc = jnp.dot(
+        img_coef.astype(jnp.bfloat16), text_all[...], preferred_element_type=jnp.float32
+    )
+    img_emb_grad = norm_backward(img_emb, img_inv, scale * img_acc)
+
+    def head_part(owner, cols):
+        return jnp.dot(
+            feat_t_blocks[owner],
+            img_emb_grad[:, cols.start : cols.start + half],
+            preferred_element_type=jnp.float32,
+        )
+
+    def grad_copy(way, m):
+        side = 0 if way == 1 else 1
+        return remote(GRAD, way, m, outgoing.at[side, m], incoming.at[side, m])
+
+    def grad_send(m):
+        for way in (1, -1):
+            side = 0 if way == 1 else 1
+            value = head_part(index_at(place + way * (n // 2 - (m + 1) // 2), n), columns(way, m))
+            if m >= 2:
+                grad_copy(way, m - 2).wait_recv()
+                value += incoming[side, m - 2].astype(jnp.float32)
+            outgoing[side, m] = value.astype(jnp.bfloat16)
+            grad_copy(way, m).start()
+
+    def text_side():
+        row_ids = lax.broadcasted_iota(jnp.int32, (pairs, rows), 0)
+        col_ids = lax.broadcasted_iota(jnp.int32, (pairs, rows), 1) + me * rows
+        label = (row_ids == col_ids).astype(jnp.float32)
+        coef = exp_all[:, own] * (inv_rows[...] + inv_cols[:, own]) - 2.0 * label
+        acc = lax.dot_general(
+            coef.astype(jnp.bfloat16), image_all[...], COLS_COLS, preferred_element_type=jnp.float32
+        )
+        text_grad_ref[...] = norm_backward(txt_emb, txt_inv, scale * acc)
+
+    def feat_side():
+        feat_grad_ref[...] = lax.dot_general(
+            img_emb_grad, head_all[...], ROWS_ROWS, preferred_element_type=jnp.float32
+        ).astype(jnp.bfloat16)
+
+    for m in range(messages):
+        grad_send(m)
+        if m == 1:
+            text_side()
+        if m == 3:
+            feat_side()
+
+    total = [head_part(me, pl.ds(0, half)), head_part(me, pl.ds(half, half))]
+    for m in range(messages - 2, messages):
+        for way in (1, -1):
+            grad_copy(way, m).wait_recv()
+            which = columns(way, m).start // half
+            total[which] += incoming[0 if way == 1 else 1, m].astype(jnp.float32)
+    head_grad_ref[:, 0:half] = total[0]
+    head_grad_ref[:, half:width] = total[1]
+
+    for m in range(messages):
+        for way in (1, -1):
+            for kind in gathered:
+                gather_copy(kind, way, m, m // 2).wait_send()
+            grad_copy(way, m).wait_send()
+
+
+def local_kernel(n, image_features, text_embed, image_head, logit_scale):
+    rows, width = text_embed.shape
+    depth, feat = image_head.shape[0], image_features.shape[1]
+    pairs = n * rows
+    half = width // 2
+    bf16, f32 = jnp.bfloat16, jnp.float32
+    vmem = pl.BlockSpec(memory_space=pltpu.VMEM)
+    return pl.pallas_call(
+        functools.partial(step_kernel, n),
+        out_shape=(
+            jax.ShapeDtypeStruct((rows, feat), bf16),
+            jax.ShapeDtypeStruct((rows, width), bf16),
+            jax.ShapeDtypeStruct((depth, width), f32),
+        ),
+        in_specs=[vmem, vmem, vmem, pl.BlockSpec(memory_space=pltpu.SMEM)],
+        out_specs=(vmem, vmem, vmem),
+        scratch_shapes=[
+            pltpu.VMEM((n * depth, width), bf16),
+            pltpu.VMEM((pairs, width), bf16),
+            pltpu.VMEM((pairs, width), bf16),
+            pltpu.VMEM((n, rows, depth), bf16),
+            pltpu.VMEM((n, depth, rows), bf16),
+            pltpu.VMEM((pairs, pairs), f32),
+            pltpu.VMEM((pairs, 1), f32),
+            pltpu.VMEM((1, pairs), f32),
+            pltpu.VMEM((2, n - 1, depth, half), bf16),
+            pltpu.VMEM((2, n - 1, depth, half), bf16),
+            pltpu.SemaphoreType.DMA((4, 2, n - 1)),
+            pltpu.SemaphoreType.DMA((4, 2, n - 1)),
+        ],
+        compiler_params=pltpu.CompilerParams(
+            collective_id=0, has_side_effects=True, vmem_limit_bytes=40 * 2**20
+        ),
+    )(image_features, text_embed, image_head, logit_scale)
+
+
+def fits_kernel(n, rows, width, depth, feat):
+    pairs = n * rows
+    size = 4 * pairs * pairs + 4 * pairs * width + 8 * n * depth * width + 12 * rows * feat
+    return (
+        n % 2 == 0
+        and n >= 6
+        and rows % 128 == 0
+        and width % 256 == 0
+        and depth % 16 == 0
+        and feat == n * depth
+        and size <= 24 * 2**20
+    )
+
+
 def solution(mesh):
-    in_specs = (P(("rep", "dp"), None), P(("rep", "dp"), None), P(("rep", "dp"), None), P())
-    out_specs = (P(("rep", "dp"), None), P(("rep", "dp"), None), P(("rep", "dp"), None))
-    return jax.shard_map(local, mesh=mesh, in_specs=in_specs, out_specs=out_specs, check_vma=False)
+    n = mesh.shape["dp"]
+    groups = mesh.shape["rep"] * n
+
+    def step(image_features, text_embed, image_head, logit_scale):
+        rows, width = text_embed.shape[0] // groups, text_embed.shape[1]
+        depth, feat = image_head.shape[0] // groups, image_features.shape[1]
+        if fits_kernel(n, rows, width, depth, feat):
+            body = functools.partial(local_kernel, n)
+        else:
+            body = local
+        split = P(("rep", "dp"), None)
+        return jax.shard_map(
+            body,
+            mesh=mesh,
+            in_specs=(split, split, split, P()),
+            out_specs=(split, split, split),
+            check_vma=False,
+        )(image_features, text_embed, image_head, logit_scale)
+
+    return step

time: 215 us -> 67.3 us (0.31)
  waiting for transfers between devices: 128 us -> 0 us
  Pallas kernels: 0 us -> 60.9 us
  blocking collectives: 53.8 us -> 0 us
  between operations: 15.1 us -> 1.3 us
  matrix products: 8.53 us -> 0 us
  other arithmetic: 4.36 us -> 0 us
    all_gather x3 -> x0, waiting for transfers between devices: 81.9 us -> none  [the longest x1 45.3 us: local(): head_full = lax.all_gather(image_head, 'dp', axis=0, tiled=True)]
    pallas_call x0 -> x1, Pallas kernels: none -> 60.9 us  [local_kernel(): pl.pallas_call(functools.partial(step_kernel, n), out_shape=(jax.ShapeDty...]
    unnamed x5 -> x0, waiting for transfers between devices: 46.2 us -> none
    all_gather x2 -> x0, blocking collectives: 34.5 us -> none  [the longest x1 18.3 us: local(): lax.all_gather(row_lse, 'dp', axis=0, tiled=True)]
    unnamed x1 -> x0, blocking collectives: 19.3 us -> none
    dot_general x6 -> x0, matrix products: 8.53 us -> none  [the longest x1 2.35 us: local(): txt_acc = jnp.dot(txt_coef, img_piece, preferred_element_type=jnp.float32)]
    convert_element_type x4 -> x0, other arithmetic: 3.33 us -> none  [the longest x1 1.65 us: local(): txt_unit = txt_scaled.astype(jnp.bfloat16)]
    unnamed x16 -> x9, local copies, waits for them, and re-layouts: 4.21 us -> 4.93 us
  transfers between devices with their start and end apart: 4 -> 0, of which waited for: 3 -> 0; matrix products, arithmetic and copies ran while one was open for 7% -> 0% of each run, Pallas kernels for 0% -> 0%
where the time goes in v1:
time: 67.3 us; the launch traced here: 67.1 us
  Pallas kernels  60.9 us (90%)
  local copies, waits for them, and re-layouts  4.93 us (7%)
  between operations  1.3 us (2%)
    pallas_call x1, Pallas kernels, local_kernel(): pl.pallas_call(functools.partial(step_kernel, n), out_shape=(jax.ShapeDty...  60.9 us
    unnamed x9, local copies, waits for them, and re-layouts  4.93 us

profile of v1, /device:TPU:0, one launch (start us, length us, event | category | flops | bytes accessed | tf_op | source)
XLA Modules:
  0.0 67.1 jit_solution(1160237422250466578)
XLA Ops:
  1.3 0.0 copy-start
  1.3 1.0 %copy-done = bf16[128,1408]{1,0:T(8,128)(2,1)S(1)} copy-done((bf16[128,1408]{1,0:T(8,128)(2,1)S(1)}, bf16[128,1408]{1,0:T(8,128)(2,1)}, u32[]{:S(2)}) %copy-start) | copy-done | bytes 360472
  2.3 0.0 copy-start.1
  2.3 0.9 %copy-done.1 = bf16[176,512]{1,0:T(8,128)(2,1)S(1)} copy-done((bf16[176,512]{1,0:T(8,128)(2,1)S(1)}, bf16[176,512]{1,0:T(8,128)(2,1)}, u32[]{:S(2)}) %copy-start.1) | copy-done | bytes 180248
  3.2 0.0 copy-start.2
  3.2 0.9 %copy-done.2 = bf16[128,512]{1,0:T(8,128)(2,1)S(1)} copy-done((bf16[128,512]{1,0:T(8,128)(2,1)S(1)}, bf16[128,512]{1,0:T(8,128)(2,1)}, u32[]{:S(2)}) %copy-start.2) | copy-done | bytes 131096
  4.1 60.9 %shard_map.67 = (bf16[128,1408]{1,0:T(8,128)(2,1)S(1)}, bf16[128,512]{1,0:T(8,128)(2,1)S(1)}, f32[176,512]{1,0:T(8,128)S(1)}) custom-call(bf16[128,1408]{1,0:T(8,128)(2,1)S(1)} %copy-done, bf16[128,512]{1,0:T(8,128)(2,1)S(1)} %copy-done.2, bf16[176,512]{1,0:T(8,128)(2,1)S(1)} %copy-done.1, f32[1]{0:T(128)S(6)} %copy.10.scale_ref), custom_call_target="tpu_custom_call" | custom-call | tf_op jit(solution)/shard_map/pallas_call | solution.py:318
  65.0 0.7 %copy.11 = bf16[128,1408]{1,0:T(8,128)(2,1)} copy(bf16[128,1408]{1,0:T(8,128)(2,1)S(1)} %get-tuple-element.6) | data formatting | bytes 720896
  65.7 0.7 copy.12
  66.4 0.7 %copy.13 = f32[176,512]{1,0:T(8,128)} copy(f32[176,512]{1,0:T(8,128)S(1)} %get-tuple-element.8) | data formatting | bytes 720896
Async XLA Ops:
  1.3 1.0 %copy-start = (bf16[128,1408]{1,0:T(8,128)(2,1)S(1)}, bf16[128,1408]{1,0:T(8,128)(2,1)}, u32[]{:S(2)}) copy-start(bf16[128,1408]{1,0:T(8,128)(2,1)} %feat_ref.1) | copy-start | bytes 1081348
  2.3 0.9 %copy-start.1 = (bf16[176,512]{1,0:T(8,128)(2,1)S(1)}, bf16[176,512]{1,0:T(8,128)(2,1)}, u32[]{:S(2)}) copy-start(bf16[176,512]{1,0:T(8,128)(2,1)} %head_ref.1) | copy-start | bytes 540676
  3.2 0.9 %copy-start.2 = (bf16[128,512]{1,0:T(8,128)(2,1)S(1)}, bf16[128,512]{1,0:T(8,128)(2,1)}, u32[]{:S(2)}) copy-start(bf16[128,512]{1,0:T(8,128)(2,1)} %text_ref.1) | copy-start | bytes 393220

commit v2 on v1

--- a/solution.py
+++ b/solution.py
@@ -88,7 +88,6 @@
 MESH = pl.DeviceIdType.MESH
 HEAD, TEXT, IMAGE, GRAD = range(4)
 ROWS_ROWS = (((1,), (1,)), ((), ()))
-COLS_COLS = (((0,), (0,)), ((), ()))
 
 
 def place_of(index, n):
@@ -104,9 +103,9 @@
 
 def step_kernel(
     n,
-    feat_ref,
-    text_ref,
-    head_ref,
+    feat_hbm,
+    text_hbm,
+    head_hbm,
     scale_ref,
     feat_grad_ref,
     text_grad_ref,
@@ -116,28 +115,43 @@
     image_all,
     feat_blocks,
     feat_t_blocks,
-    exp_all,
-    inv_rows,
+    feat_ref,
+    text_ref,
+    exp_blocks,
+    stats,
     inv_cols,
     outgoing,
     incoming,
+    load_sem,
     send_sem,
     recv_sem,
+    stats_send_sem,
+    stats_recv_sem,
 ):
-    rows, width = text_ref.shape
-    depth = head_ref.shape[0]
+    rows, width = text_hbm.shape
+    depth = head_hbm.shape[0]
+    pairs = n * rows
     half = width // 2
     messages = n - 1
     me = lax.axis_index("dp")
     place = place_of(me, n)
     partner = {+1: index_at(place + 1, n), -1: index_at(place - 1, n)}
 
+    own_head = head_all.at[pl.ds(pl.multiple_of(me * depth, 16), depth), :]
+    loads = [
+        pltpu.make_async_copy(head_hbm, own_head, load_sem.at[0]),
+        pltpu.make_async_copy(text_hbm, text_ref, load_sem.at[1]),
+        pltpu.make_async_copy(feat_hbm, feat_ref, load_sem.at[2]),
+    ]
+    for load in loads:
+        load.start()
     barrier = pltpu.get_barrier_semaphore()
-    for way in (1, -1):
-        pl.semaphore_signal(barrier, inc=1, device_id={"dp": partner[way]}, device_id_type=MESH)
-
-    head_all[pl.ds(pl.multiple_of(me * depth, 16), depth), :] = head_ref[...]
-    pl.semaphore_wait(barrier, 2)
+    for k in range(1, n):
+        pl.semaphore_signal(
+            barrier, inc=1, device_id={"dp": lax.rem(me + k, n)}, device_id_type=MESH
+        )
+    loads[0].wait()
+    pl.semaphore_wait(barrier, n - 1)
 
     def columns(way, m):
         first = (m % 2 == 0) == (way == 1)
@@ -176,9 +190,11 @@
     gather_send(HEAD, 0)
     gather_send(HEAD, 1)
 
+    loads[1].wait()
     txt_emb = text_ref[...].astype(jnp.float32)
     txt_scaled, txt_inv = unit_rows(txt_emb)
     text_all[pl.ds(pl.multiple_of(me * rows, 16), rows), :] = txt_scaled.astype(jnp.bfloat16)
+    loads[2].wait()
     feat_t = feat_ref[...].astype(jnp.float32).T
     for b in range(n):
         block = feat_t[b * depth : (b + 1) * depth]
@@ -205,45 +221,62 @@
         img_emb += emb_part(index_at(place - way * (n // 2 - 1), n))
     img_emb += emb_part(index_at(place + n // 2, n))
     img_scaled, img_inv = unit_rows(img_emb)
-    image_all[pl.ds(pl.multiple_of(me * rows, 16), rows), :] = img_scaled.astype(jnp.bfloat16)
-
-    for m in range(messages - 2):
-        gather_send(IMAGE, m)
-        gather_send(TEXT, m + 2)
+    img_unit = img_scaled.astype(jnp.bfloat16)
+    image_all[pl.ds(pl.multiple_of(me * rows, 16), rows), :] = img_unit
+
+    scale = scale_ref[0]
+
+    def exp_block(owner):
+        at = pl.ds(pl.multiple_of(owner * rows, 16), rows)
+        exp_blocks[owner] = jnp.exp(tile_logits(scale, img_unit, text_all[at, :]))
+
+    image_sent = 0
+    for m in range(2, messages):
+        gather_send(TEXT, m)
+        if m % 2 == 0 and image_sent < 2:
+            gather_send(IMAGE, image_sent)
+            image_sent += 1
+        if m == 2:
+            exp_block(me)
+        if m % 2 == 1:
+            for way in (1, -1):
+                exp_block(index_at(place - way * (m // 2), n))
     gather_last(TEXT)
-
-    scale = scale_ref[0]
-
-    def exp_block(owner, col_sum):
-        at = pl.ds(pl.multiple_of(owner * rows, 16), rows)
-        values = jnp.exp(
-            scale
-            * lax.dot_general(
-                image_all[at, :], text_all[...], ROWS_ROWS, preferred_element_type=jnp.float32
-            )
-        )
-        exp_all[at, :] = values
-        inv_rows[at, :] = 1.0 / jnp.sum(values, axis=1, keepdims=True)
-        return col_sum + jnp.sum(values, axis=0, keepdims=True)
-
-    col_sum = exp_block(me, jnp.zeros((1, n * rows), jnp.float32))
-    for shift in range(1, n // 2):
-        m = messages - 2 + (shift - 1)
-        if m < messages:
-            gather_send(IMAGE, m)
-        if shift == n // 2 - 1:
-            gather_last(IMAGE)
-        for way in (1, -1):
-            col_sum = exp_block(index_at(place - way * shift, n), col_sum)
-    col_sum = exp_block(index_at(place + n // 2, n), col_sum)
+    for way in (1, -1):
+        exp_block(index_at(place - way * (n // 2 - 1), n))
+    exp_block(index_at(place + n // 2, n))
+
+    exp_rows = jnp.concatenate([exp_blocks[b] for b in range(n)], axis=1)
+    row_sum = jnp.sum(exp_rows, axis=1, keepdims=True)
+    stats[me, :, 0:pairs] = jnp.sum(exp_rows, axis=0, keepdims=True)
+    stats[me, :, pairs : pairs + rows] = jnp.broadcast_to(row_sum, (rows, rows)).T[0:1, :]
+
+    def stats_copy(k, sender):
+        return pltpu.make_async_remote_copy(
+            src_ref=stats.at[sender],
+            dst_ref=stats.at[sender],
+            send_sem=stats_send_sem.at[k - 1],
+            recv_sem=stats_recv_sem.at[k - 1],
+            device_id={"dp": lax.rem(me + k, n)},
+            device_id_type=MESH,
+        )
+
+    for k in range(1, n):
+        stats_copy(k, me).start()
+    while image_sent < messages - 2:
+        gather_send(IMAGE, image_sent)
+        image_sent += 1
+    for k in range(1, n):
+        stats_copy(k, lax.rem(me - k + n, n)).wait_recv()
+
+    col_sum = stats[0, :, 0:pairs]
+    for b in range(1, n):
+        col_sum += stats[b, :, 0:pairs]
     inv_col = 1.0 / col_sum
     inv_cols[...] = inv_col
-
-    own = pl.ds(pl.multiple_of(me * rows, 128), rows)
-    pairs = n * rows
     row_ids = lax.broadcasted_iota(jnp.int32, (rows, pairs), 0) + me * rows
     label = (row_ids == lax.broadcasted_iota(jnp.int32, (rows, pairs), 1)).astype(jnp.float32)
-    img_coef = exp_all[own, :] * (inv_rows[own, :] + inv_col) - 2.0 * label
+    img_coef = exp_rows * (1.0 / row_sum + inv_col) - 2.0 * label
     img_acc = jnp.dot(
         img_coef.astype(jnp.bfloat16), text_all[...], preferred_element_type=jnp.float32
     )
@@ -271,12 +304,16 @@
             grad_copy(way, m).start()
 
     def text_side():
-        row_ids = lax.broadcasted_iota(jnp.int32, (pairs, rows), 0)
-        col_ids = lax.broadcasted_iota(jnp.int32, (pairs, rows), 1) + me * rows
-        label = (row_ids == col_ids).astype(jnp.float32)
-        coef = exp_all[:, own] * (inv_rows[...] + inv_cols[:, own]) - 2.0 * label
-        acc = lax.dot_general(
-            coef.astype(jnp.bfloat16), image_all[...], COLS_COLS, preferred_element_type=jnp.float32
+        own = pl.ds(pl.multiple_of(me * rows, 128), rows)
+        own_text = text_all[pl.ds(pl.multiple_of(me * rows, 16), rows), :]
+        exp_texts = jnp.exp(tile_logits(scale, own_text, image_all[...]))
+        inv_row = 1.0 / jnp.concatenate(
+            [stats[b, :, pairs : pairs + rows] for b in range(n)], axis=1
+        )
+        inv_own = jnp.broadcast_to(inv_cols[:, own], (rows, rows)).T[:, 0:1]
+        coef = exp_texts * (inv_own + inv_row) - 2.0 * label
+        acc = jnp.dot(
+            coef.astype(jnp.bfloat16), image_all[...], preferred_element_type=jnp.float32
         )
         text_grad_ref[...] = norm_backward(txt_emb, txt_inv, scale * acc)
 
@@ -287,10 +324,14 @@
 
     for m in range(messages):
         grad_send(m)
-        if m == 1:
+        if m >= 1 and image_sent < messages:
+            gather_send(IMAGE, image_sent)
+            image_sent += 1
+        if m == 2:
+            feat_side()
+        if m == messages - 2:
+            gather_last(IMAGE)
             text_side()
-        if m == 3:
-            feat_side()
 
     total = [head_part(me, pl.ds(0, half)), head_part(me, pl.ds(half, half))]
     for m in range(messages - 2, messages):
@@ -306,6 +347,8 @@
             for kind in gathered:
                 gather_copy(kind, way, m, m // 2).wait_send()
             grad_copy(way, m).wait_send()
+    for k in range(1, n):
+        stats_copy(k, me).wait_send()
 
 
 def local_kernel(n, image_features, text_embed, image_head, logit_scale):
@@ -315,6 +358,7 @@
     half = width // 2
     bf16, f32 = jnp.bfloat16, jnp.float32
     vmem = pl.BlockSpec(memory_space=pltpu.VMEM)
+    hbm = pl.BlockSpec(memory_space=pltpu.HBM)
     return pl.pallas_call(
         functools.partial(step_kernel, n),
         out_shape=(
@@ -322,7 +366,7 @@
             jax.ShapeDtypeStruct((rows, width), bf16),
             jax.ShapeDtypeStruct((depth, width), f32),
         ),
-        in_specs=[vmem, vmem, vmem, pl.BlockSpec(memory_space=pltpu.SMEM)],
+        in_specs=[hbm, hbm, hbm, pl.BlockSpec(memory_space=pltpu.SMEM)],
         out_specs=(vmem, vmem, vmem),
         scratch_shapes=[
             pltpu.VMEM((n * depth, width), bf16),
@@ -330,23 +374,28 @@
             pltpu.VMEM((pairs, width), bf16),
             pltpu.VMEM((n, rows, depth), bf16),
             pltpu.VMEM((n, depth, rows), bf16),
-            pltpu.VMEM((pairs, pairs), f32),
-            pltpu.VMEM((pairs, 1), f32),
+            pltpu.VMEM((rows, feat), bf16),
+            pltpu.VMEM((rows, width), bf16),
+            pltpu.VMEM((n, rows, rows), f32),
+            pltpu.VMEM((n, 1, pairs + rows), f32),
             pltpu.VMEM((1, pairs), f32),
             pltpu.VMEM((2, n - 1, depth, half), bf16),
             pltpu.VMEM((2, n - 1, depth, half), bf16),
+            pltpu.SemaphoreType.DMA((3,)),
             pltpu.SemaphoreType.DMA((4, 2, n - 1)),
             pltpu.SemaphoreType.DMA((4, 2, n - 1)),
+            pltpu.SemaphoreType.DMA((n - 1,)),
+            pltpu.SemaphoreType.DMA((n - 1,)),
         ],
         compiler_params=pltpu.CompilerParams(
-            collective_id=0, has_side_effects=True, vmem_limit_bytes=40 * 2**20
+            collective_id=0, has_side_effects=True, vmem_limit_bytes=62 * 2**20
         ),
     )(image_features, text_embed, image_head, logit_scale)
 
 
 def fits_kernel(n, rows, width, depth, feat):
     pairs = n * rows
-    size = 4 * pairs * pairs + 4 * pairs * width + 8 * n * depth * width + 12 * rows * feat
+    size = 24 * pairs * rows + 4 * pairs * width + 8 * n * depth * width + 12 * rows * feat
     return (
         n % 2 == 0
         and n >= 6

time: 67.3 us -> 66.2 us (0.984)
  local copies, waits for them, and re-layouts: 4.93 us -> 3.2 us
  Pallas kernels: 60.9 us -> 61.6 us
    unnamed x9 -> x7, local copies, waits for them, and re-layouts: 4.93 us -> 3.2 us
    pallas_call x1, Pallas kernels: 60.9 us -> 61.6 us  [local_kernel(): pl.pallas_call(functools.partial(step_kernel, n), out_shape=(jax.ShapeDty...]
where the time goes in v2:
time: 66.2 us; the launch traced here: 66.1 us
  Pallas kernels  61.6 us (93%)
  local copies, waits for them, and re-layouts  3.2 us (5%)
  between operations  1.3 us (2%)
    pallas_call x1, Pallas kernels, local_kernel(): pl.pallas_call(functools.partial(step_kernel, n), out_shape=(jax.ShapeDty...  61.6 us
    unnamed x7, local copies, waits for them, and re-layouts  3.2 us

profile of v2, /device:TPU:0, one launch (start us, length us, event | category | flops | bytes accessed | tf_op | source)
XLA Modules:
  0.0 66.1 jit_solution(11904905723342710712)
XLA Ops:
  1.3 61.6 %shard_map.67 = (bf16[128,1408]{1,0:T(8,128)(2,1)}, bf16[128,512]{1,0:T(8,128)(2,1)}, f32[176,512]{1,0:T(8,128)}) custom-call(bf16[128,1408]{1,0:T(8,128)(2,1)} %feat_hbm.1, bf16[128,512]{1,0:T(8,128)(2,1)} %text_hbm.1, bf16[176,512]{1,0:T(8,128)(2,1)} %head_hbm.1, f32[1]{0:T(128)S(6)} %copy.10.scale_ref), custom_call_target="tpu_custom_call" | custom-call | tf_op jit(solution)/shard_map/pallas_call | solution.py:362
  62.8 0.0 copy-start.1
  62.9 0.0 copy-start
  62.9 1.8 %copy.11 = bf16[128,1408]{1,0:T(8,128)(2,1)} copy(bf16[128,1408]{1,0:T(8,128)(2,1)} %get-tuple-element.6) | data formatting | bytes 720896
  64.7 0.0 copy-done.1
  64.7 0.7 copy.12
  65.3 0.0 copy-done
  65.3 0.7 %copy.13 = f32[176,512]{1,0:T(8,128)} copy(f32[176,512]{1,0:T(8,128)S(1)} %copy-done) | data formatting | bytes 720896
Async XLA Ops:
  62.8 1.8 %copy-start.1 = (bf16[128,512]{1,0:T(8,128)(2,1)S(1)}, bf16[128,512]{1,0:T(8,128)(2,1)}, u32[]{:S(2)}) copy-start(bf16[128,512]{1,0:T(8,128)(2,1)} %get-tuple-element.7) | copy-start | bytes 393220
  62.9 2.5 %copy-start = (f32[176,512]{1,0:T(8,128)S(1)}, f32[176,512]{1,0:T(8,128)}, u32[]{:S(2)}) copy-start(f32[176,512]{1,0:T(8,128)} %get-tuple-element.8) | copy-start | bytes 1081348

commit v3 on v2

--- a/solution.py
+++ b/solution.py
@@ -107,6 +107,9 @@
     text_hbm,
     head_hbm,
     scale_ref,
+    feat_out,
+    text_out,
+    head_out,
     feat_grad_ref,
     text_grad_ref,
     head_grad_ref,
@@ -123,6 +126,7 @@
     outgoing,
     incoming,
     load_sem,
+    store_sem,
     send_sem,
     recv_sem,
     stats_send_sem,
@@ -142,6 +146,11 @@
         pltpu.make_async_copy(head_hbm, own_head, load_sem.at[0]),
         pltpu.make_async_copy(text_hbm, text_ref, load_sem.at[1]),
         pltpu.make_async_copy(feat_hbm, feat_ref, load_sem.at[2]),
+    ]
+    stores = [
+        pltpu.make_async_copy(feat_grad_ref, feat_out, store_sem.at[0]),
+        pltpu.make_async_copy(text_grad_ref, text_out, store_sem.at[1]),
+        pltpu.make_async_copy(head_grad_ref, head_out, store_sem.at[2]),
     ]
     for load in loads:
         load.start()
@@ -316,11 +325,13 @@
             coef.astype(jnp.bfloat16), image_all[...], preferred_element_type=jnp.float32
         )
         text_grad_ref[...] = norm_backward(txt_emb, txt_inv, scale * acc)
+        stores[1].start()
 
     def feat_side():
         feat_grad_ref[...] = lax.dot_general(
             img_emb_grad, head_all[...], ROWS_ROWS, preferred_element_type=jnp.float32
         ).astype(jnp.bfloat16)
+        stores[0].start()
 
     for m in range(messages):
         grad_send(m)
@@ -341,6 +352,7 @@
             total[which] += incoming[0 if way == 1 else 1, m].astype(jnp.float32)
     head_grad_ref[:, 0:half] = total[0]
     head_grad_ref[:, half:width] = total[1]
+    stores[2].start()
 
     for m in range(messages):
         for way in (1, -1):
@@ -349,6 +361,20 @@
             grad_copy(way, m).wait_send()
     for k in range(1, n):
         stats_copy(k, me).wait_send()
+    for store in stores:
+        store.wait()
+
+
+def hand_on_kernel(*refs):
+    sources, results, sem = refs[:3], refs[3:6], refs[6]
+    copies = [
+        pltpu.make_async_copy(source, result, sem.at[i])
+        for i, (source, result) in enumerate(zip(sources, results))
+    ]
+    for copy in copies:
+        copy.start()
+    for copy in copies:
+        copy.wait()
 
 
 def local_kernel(n, image_features, text_embed, image_head, logit_scale):
@@ -357,18 +383,21 @@
     pairs = n * rows
     half = width // 2
     bf16, f32 = jnp.bfloat16, jnp.float32
-    vmem = pl.BlockSpec(memory_space=pltpu.VMEM)
     hbm = pl.BlockSpec(memory_space=pltpu.HBM)
-    return pl.pallas_call(
+    out_shape = (
+        jax.ShapeDtypeStruct((rows, feat), bf16),
+        jax.ShapeDtypeStruct((rows, width), bf16),
+        jax.ShapeDtypeStruct((depth, width), f32),
+    )
+    results = pl.pallas_call(
         functools.partial(step_kernel, n),
-        out_shape=(
-            jax.ShapeDtypeStruct((rows, feat), bf16),
-            jax.ShapeDtypeStruct((rows, width), bf16),
-            jax.ShapeDtypeStruct((depth, width), f32),
-        ),
+        out_shape=out_shape,
         in_specs=[hbm, hbm, hbm, pl.BlockSpec(memory_space=pltpu.SMEM)],
-        out_specs=(vmem, vmem, vmem),
+        out_specs=(hbm, hbm, hbm),
         scratch_shapes=[
+            pltpu.VMEM((rows, feat), bf16),
+            pltpu.VMEM((rows, width), bf16),
+            pltpu.VMEM((depth, width), f32),
             pltpu.VMEM((n * depth, width), bf16),
             pltpu.VMEM((pairs, width), bf16),
             pltpu.VMEM((pairs, width), bf16),
@@ -382,6 +411,7 @@
             pltpu.VMEM((2, n - 1, depth, half), bf16),
             pltpu.VMEM((2, n - 1, depth, half), bf16),
             pltpu.SemaphoreType.DMA((3,)),
+            pltpu.SemaphoreType.DMA((3,)),
             pltpu.SemaphoreType.DMA((4, 2, n - 1)),
             pltpu.SemaphoreType.DMA((4, 2, n - 1)),
             pltpu.SemaphoreType.DMA((n - 1,)),
@@ -391,6 +421,14 @@
             collective_id=0, has_side_effects=True, vmem_limit_bytes=62 * 2**20
         ),
     )(image_features, text_embed, image_head, logit_scale)
+    return pl.pallas_call(
+        hand_on_kernel,
+        out_shape=out_shape,
+        in_specs=[hbm, hbm, hbm],
+        out_specs=(hbm, hbm, hbm),
+        scratch_shapes=[pltpu.SemaphoreType.DMA((3,))],
+        compiler_params=pltpu.CompilerParams(vmem_limit_bytes=62 * 2**20),
+    )(*results)
 
 
 def fits_kernel(n, rows, width, depth, feat):

time: 66.2 us -> 89.7 us (1.35)
  Pallas kernels: 61.6 us -> 88.3 us
  local copies, waits for them, and re-layouts: 3.2 us -> 0 us
    pallas_call x1 -> x2, Pallas kernels: 61.6 us -> 88.3 us  [the longest x1 61.3 us: local_kernel(): pl.pallas_call(functools.partial(step_kernel, n), out_shape=out_shape, in...]
    unnamed x7 -> x0, local copies, waits for them, and re-layouts: 3.2 us -> none
where the time goes in v3:
time: 89.7 us; the launch traced here: 89.5 us
  Pallas kernels  88.3 us (98%)
  between operations  1.29 us (1%)
    pallas_call x1, Pallas kernels, local_kernel(): pl.pallas_call(functools.partial(step_kernel, n), out_shape=out_shape, in...  61.3 us
    pallas_call x1, Pallas kernels, local_kernel(): pl.pallas_call(hand_on_kernel, out_shape=out_shape, in_specs=[hbm, hbm, h...  26.9 us

profile of v3, /device:TPU:0, one launch (start us, length us, event | category | flops | bytes accessed | tf_op | source)
XLA Modules:
  0.0 89.5 jit_solution(11116809500491382900)
XLA Ops:
  1.3 61.3 %shard_map.67 = (bf16[128,1408]{1,0:T(8,128)(2,1)}, bf16[128,512]{1,0:T(8,128)(2,1)}, f32[176,512]{1,0:T(8,128)}) custom-call(bf16[128,1408]{1,0:T(8,128)(2,1)} %feat_hbm.1, bf16[128,512]{1,0:T(8,128)(2,1)} %text_hbm.1, bf16[176,512]{1,0:T(8,128)(2,1)} %head_hbm.1, f32[1]{0:T(128)S(6)} %copy.7.scale_ref), custom_call_target="tpu_custom_call" | custom-call | tf_op jit(solution)/shard_map/pallas_call | solution.py:392
  62.6 26.9 %shard_map.68 = (bf16[128,1408]{1,0:T(8,128)(2,1)}, bf16[128,512]{1,0:T(8,128)(2,1)}, f32[176,512]{1,0:T(8,128)}) custom-call(bf16[128,1408]{1,0:T(8,128)(2,1)} %get-tuple-element.6.refs_0_, bf16[128,512]{1,0:T(8,128)(2,1)} %get-tuple-element.7.refs_1_, f32[176,512]{1,0:T(8,128)} %get-tuple-element.8.refs_2_), custom_call_target="tpu_custom_call" | custom-call | tf_op jit(solution)/shard_map/pallas_call | solution.py:424

commit v4 on v3

--- a/solution.py
+++ b/solution.py
@@ -86,8 +86,10 @@
 
 
 MESH = pl.DeviceIdType.MESH
-HEAD, TEXT, IMAGE, GRAD = range(4)
+HEAD, GRAD = range(2)
+IMAGES, IMAGE_GRADS, ROW_SUMS = range(3)
 ROWS_ROWS = (((1,), (1,)), ((), ()))
+COLS_COLS = (((0,), (0,)), ((), ()))
 
 
 def place_of(index, n):
@@ -114,31 +116,42 @@
     text_grad_ref,
     head_grad_ref,
     head_all,
-    text_all,
-    image_all,
+    text_col,
+    images,
     feat_blocks,
     feat_t_blocks,
     feat_ref,
     text_ref,
-    exp_blocks,
-    stats,
-    inv_cols,
+    coefs,
+    row_stats,
+    col_stats,
+    image_out,
+    image_in,
+    text_part,
+    text_going,
+    text_coming,
     outgoing,
     incoming,
     load_sem,
     store_sem,
     send_sem,
     recv_sem,
+    pair_send_sem,
+    pair_recv_sem,
     stats_send_sem,
     stats_recv_sem,
+    chain_send_sem,
+    chain_recv_sem,
 ):
     rows, width = text_hbm.shape
     depth = head_hbm.shape[0]
-    pairs = n * rows
     half = width // 2
+    length = n // 2
     messages = n - 1
     me = lax.axis_index("dp")
     place = place_of(me, n)
+    level, side = lax.div(me, 2), lax.rem(me, 2)
+    other = me + 1 - 2 * side
     partner = {+1: index_at(place + 1, n), -1: index_at(place - 1, n)}
 
     own_head = head_all.at[pl.ds(pl.multiple_of(me * depth, 16), depth), :]
@@ -177,7 +190,7 @@
             device_id_type=MESH,
         )
 
-    gathered = {HEAD: (head_all, depth), TEXT: (text_all, rows), IMAGE: (image_all, rows)}
+    gathered = {HEAD: (head_all, depth)}
 
     def gather_copy(kind, way, m, origin_shift):
         buf, block = gathered[kind]
@@ -196,13 +209,63 @@
             for way in (1, -1):
                 gather_copy(kind, way, m, m // 2 + 1).wait_recv()
 
+    def along(way):
+        return level if way == 1 else length - 1 - level
+
+    def chain_copy(kind, way, slot, src, dst):
+        return pltpu.make_async_remote_copy(
+            src_ref=src,
+            dst_ref=dst,
+            send_sem=chain_send_sem.at[kind, 0 if way == 1 else 1, slot],
+            recv_sem=chain_recv_sem.at[kind, 0 if way == 1 else 1, slot],
+            device_id={"dp": lax.rem(me + 2 * way + n, n)},
+            device_id_type=MESH,
+        )
+
+    def text_copy(way, slot, shift):
+        owner = level - way * shift
+        ref = text_col.at[pl.ds(pl.multiple_of(owner * rows, 16), rows), :]
+        return chain_copy(0, way, slot, ref, ref)
+
+    def text_slot(slot):
+        for way in (1, -1):
+            if slot >= 1:
+
+                @pl.when(along(way) >= slot)
+                def _():
+                    text_copy(way, slot - 1, slot).wait_recv()
+
+            if slot <= length - 2:
+
+                @pl.when((along(way) >= slot) & (along(way) < length - 1))
+                def _():
+                    text_copy(way, slot, slot).start()
+
+    def pair_copy(kind, src, dst):
+        return pltpu.make_async_remote_copy(
+            src_ref=src,
+            dst_ref=dst,
+            send_sem=pair_send_sem.at[kind],
+            recv_sem=pair_recv_sem.at[kind],
+            device_id={"dp": other},
+            device_id_type=MESH,
+        )
+
+    own_images = pl.ds(pl.multiple_of(side * rows, 16), rows)
+    other_images = pl.ds(pl.multiple_of((1 - side) * rows, 16), rows)
+    images_copy = pair_copy(IMAGES, images.at[own_images, :], images.at[own_images, :])
+    images_landed = pair_copy(IMAGES, images.at[other_images, :], images.at[other_images, :])
+    grads_copy = pair_copy(IMAGE_GRADS, image_out, image_in)
+    sums_copy = pair_copy(ROW_SUMS, row_stats.at[side], row_stats.at[side])
+    sums_landed = pair_copy(ROW_SUMS, row_stats.at[1 - side], row_stats.at[1 - side])
+
     gather_send(HEAD, 0)
     gather_send(HEAD, 1)
 
     loads[1].wait()
     txt_emb = text_ref[...].astype(jnp.float32)
     txt_scaled, txt_inv = unit_rows(txt_emb)
-    text_all[pl.ds(pl.multiple_of(me * rows, 16), rows), :] = txt_scaled.astype(jnp.bfloat16)
+    text_col[pl.ds(pl.multiple_of(level * rows, 16), rows), :] = txt_scaled.astype(jnp.bfloat16)
     loads[2].wait()
     feat_t = feat_ref[...].astype(jnp.float32).T
     for b in range(n):
@@ -223,72 +286,98 @@
         if m % 2 == 1:
             for way in (1, -1):
                 img_emb += emb_part(index_at(place - way * (m // 2), n))
-    gather_send(TEXT, 0)
-    gather_send(TEXT, 1)
+        if m == messages - 2:
+            text_slot(0)
     gather_last(HEAD)
+    text_slot(1)
     for way in (1, -1):
         img_emb += emb_part(index_at(place - way * (n // 2 - 1), n))
     img_emb += emb_part(index_at(place + n // 2, n))
     img_scaled, img_inv = unit_rows(img_emb)
     img_unit = img_scaled.astype(jnp.bfloat16)
-    image_all[pl.ds(pl.multiple_of(me * rows, 16), rows), :] = img_unit
+    images[own_images, :] = img_unit
+    images_copy.start()
+    for slot in range(2, length):
+        text_slot(slot)
 
     scale = scale_ref[0]
-
-    def exp_block(owner):
-        at = pl.ds(pl.multiple_of(owner * rows, 16), rows)
-        exp_blocks[owner] = jnp.exp(tile_logits(scale, img_unit, text_all[at, :]))
-
-    image_sent = 0
-    for m in range(2, messages):
-        gather_send(TEXT, m)
-        if m % 2 == 0 and image_sent < 2:
-            gather_send(IMAGE, image_sent)
-            image_sent += 1
-        if m == 2:
-            exp_block(me)
-        if m % 2 == 1:
-            for way in (1, -1):
-                exp_block(index_at(place - way * (m // 2), n))
-    gather_last(TEXT)
-    for way in (1, -1):
-        exp_block(index_at(place - way * (n // 2 - 1), n))
-    exp_block(index_at(place + n // 2, n))
-
-    exp_rows = jnp.concatenate([exp_blocks[b] for b in range(n)], axis=1)
-    row_sum = jnp.sum(exp_rows, axis=1, keepdims=True)
-    stats[me, :, 0:pairs] = jnp.sum(exp_rows, axis=0, keepdims=True)
-    stats[me, :, pairs : pairs + rows] = jnp.broadcast_to(row_sum, (rows, rows)).T[0:1, :]
+    images_landed.wait_recv()
+    exp_tile = jnp.exp(tile_logits(scale, images[...], text_col[...]))
+    row_part = jnp.sum(exp_tile, axis=1, keepdims=True)
+    row_stats[side] = jnp.broadcast_to(row_part, (2 * rows, rows)).T[0:1, :]
+    col_stats[level] = jnp.sum(exp_tile, axis=0, keepdims=True)
 
     def stats_copy(k, sender):
         return pltpu.make_async_remote_copy(
-            src_ref=stats.at[sender],
-            dst_ref=stats.at[sender],
+            src_ref=col_stats.at[sender],
+            dst_ref=col_stats.at[sender],
             send_sem=stats_send_sem.at[k - 1],
             recv_sem=stats_recv_sem.at[k - 1],
-            device_id={"dp": lax.rem(me + k, n)},
+            device_id={"dp": 2 * lax.rem(level + k, length) + side},
             device_id_type=MESH,
         )
 
-    for k in range(1, n):
-        stats_copy(k, me).start()
-    while image_sent < messages - 2:
-        gather_send(IMAGE, image_sent)
-        image_sent += 1
-    for k in range(1, n):
-        stats_copy(k, lax.rem(me - k + n, n)).wait_recv()
-
-    col_sum = stats[0, :, 0:pairs]
-    for b in range(1, n):
-        col_sum += stats[b, :, 0:pairs]
-    inv_col = 1.0 / col_sum
-    inv_cols[...] = inv_col
-    row_ids = lax.broadcasted_iota(jnp.int32, (rows, pairs), 0) + me * rows
-    label = (row_ids == lax.broadcasted_iota(jnp.int32, (rows, pairs), 1)).astype(jnp.float32)
-    img_coef = exp_rows * (1.0 / row_sum + inv_col) - 2.0 * label
+    for k in range(1, length):
+        stats_copy(k, level).start()
+    sums_copy.start()
+    sums_landed.wait_recv()
+    inv_row = 1.0 / jnp.broadcast_to(row_stats[0] + row_stats[1], (rows, 2 * rows)).T[:, 0:1]
+    tile = (2 * rows, length * rows)
+    row_ids = lax.broadcasted_iota(jnp.int32, tile, 0) - side * rows
+    col_ids = lax.broadcasted_iota(jnp.int32, tile, 1) - level * rows
+    label = (row_ids == col_ids) & (row_ids >= 0) & (row_ids < rows)
+    minus = jnp.where(label, 2.0, 0.0)
+    for k in range(1, length):
+        stats_copy(k, lax.rem(level - k + length, length)).wait_recv()
+    col_sum = col_stats[0]
+    for k in range(1, length):
+        col_sum += col_stats[k]
+    coefs[...] = (exp_tile * (inv_row + 1.0 / col_sum) - minus).astype(jnp.bfloat16)
+
+    image_out[...] = jnp.dot(
+        coefs[other_images, :], text_col[...], preferred_element_type=jnp.float32
+    ).astype(jnp.bfloat16)
+    grads_copy.start()
+    text_acc = lax.dot_general(
+        coefs[...], images[...], COLS_COLS, preferred_element_type=jnp.float32
+    )
+    for b in range(length):
+        text_part[b] = text_acc[b * rows : (b + 1) * rows]
+
+    def text_grad_copy(way, slot):
+        which = 0 if way == 1 else 1
+        return chain_copy(1, way, slot, text_going.at[which, slot], text_coming.at[which, slot])
+
+    def text_grad_slot(slot):
+        for way in (1, -1):
+            which = 0 if way == 1 else 1
+
+            @pl.when(along(way) <= slot)
+            def _():
+                ahead = length - 1 - slot + along(way)
+                value = text_part[ahead if way == 1 else length - 1 - ahead]
+                text_going[which, slot] = value.astype(jnp.bfloat16)
+
+            if slot >= 1:
+
+                @pl.when((along(way) <= slot) & (along(way) >= 1))
+                def _():
+                    ahead = length - 1 - slot + along(way)
+                    value = text_part[ahead if way == 1 else length - 1 - ahead]
+                    text_grad_copy(way, slot - 1).wait_recv()
+                    value += text_coming[which, slot - 1].astype(jnp.float32)
+                    text_going[which, slot] = value.astype(jnp.bfloat16)
+
+            @pl.when(along(way) <= slot)
+            def _():
+                text_grad_copy(way, slot).start()
+
+    text_grad_slot(0)
     img_acc = jnp.dot(
-        img_coef.astype(jnp.bfloat16), text_all[...], preferred_element_type=jnp.float32
-    )
+        coefs[own_images, :], text_col[...], preferred_element_type=jnp.float32
+    )
+    grads_copy.wait_recv()
+    img_acc += image_in[...].astype(jnp.float32)
     img_emb_grad = norm_backward(img_emb, img_inv, scale * img_acc)
 
     def head_part(owner, cols):
@@ -313,18 +402,15 @@
             grad_copy(way, m).start()
 
     def text_side():
-        own = pl.ds(pl.multiple_of(me * rows, 128), rows)
-        own_text = text_all[pl.ds(pl.multiple_of(me * rows, 16), rows), :]
-        exp_texts = jnp.exp(tile_logits(scale, own_text, image_all[...]))
-        inv_row = 1.0 / jnp.concatenate(
-            [stats[b, :, pairs : pairs + rows] for b in range(n)], axis=1
-        )
-        inv_own = jnp.broadcast_to(inv_cols[:, own], (rows, rows)).T[:, 0:1]
-        coef = exp_texts * (inv_own + inv_row) - 2.0 * label
-        acc = jnp.dot(
-            coef.astype(jnp.bfloat16), image_all[...], preferred_element_type=jnp.float32
-        )
-        text_grad_ref[...] = norm_backward(txt_emb, txt_inv, scale * acc)
+        for way in (1, -1):
+            which = 0 if way == 1 else 1
+
+            @pl.when(along(way) >= 1)
+            def _():
+                text_grad_copy(way, length - 2).wait_recv()
+                text_part[level] += text_coming[which, length - 2].astype(jnp.float32)
+
+        text_grad_ref[...] = norm_backward(txt_emb, txt_inv, scale * text_part[level])
         stores[1].start()
 
     def feat_side():
@@ -335,13 +421,11 @@
 
     for m in range(messages):
         grad_send(m)
-        if m >= 1 and image_sent < messages:
-            gather_send(IMAGE, image_sent)
-            image_sent += 1
-        if m == 2:
+        if m >= 1 and m <= length - 2:
+            text_grad_slot(m)
+        if m == length - 1:
             feat_side()
         if m == messages - 2:
-            gather_last(IMAGE)
             text_side()
 
     total = [head_part(me, pl.ds(0, half)), head_part(me, pl.ds(half, half))]
@@ -359,28 +443,43 @@
             for kind in gathered:
                 gather_copy(kind, way, m, m // 2).wait_send()
             grad_copy(way, m).wait_send()
-    for k in range(1, n):
-        stats_copy(k, me).wait_send()
+    for k in range(1, length):
+        stats_copy(k, level).wait_send()
+    images_copy.wait_send()
+    grads_copy.wait_send()
+    sums_copy.wait_send()
+    for way in (1, -1):
+        for slot in range(length - 1):
+
+            @pl.when((along(way) >= slot) & (along(way) < length - 1))
+            def _():
+                text_copy(way, slot, slot).wait_send()
+
+            @pl.when(along(way) <= slot)
+            def _():
+                text_grad_copy(way, slot).wait_send()
+
     for store in stores:
         store.wait()
 
 
 def hand_on_kernel(*refs):
-    sources, results, sem = refs[:3], refs[3:6], refs[6]
-    copies = [
-        pltpu.make_async_copy(source, result, sem.at[i])
-        for i, (source, result) in enumerate(zip(sources, results))
-    ]
-    for copy in copies:
-        copy.start()
-    for copy in copies:
-        copy.wait()
+    sources, results, held, sem = refs[:3], refs[3:6], refs[6:9], refs[9]
+    loads = [pltpu.make_async_copy(sources[i], held[i], sem.at[0, i]) for i in range(3)]
+    stores = [pltpu.make_async_copy(held[i], results[i], sem.at[1, i]) for i in range(3)]
+    for load in loads:
+        load.start()
+    for load, store in zip(loads, stores):
+        load.wait()
+        store.start()
+    for store in stores:
+        store.wait()
 
 
 def local_kernel(n, image_features, text_embed, image_head, logit_scale):
     rows, width = text_embed.shape
     depth, feat = image_head.shape[0], image_features.shape[1]
-    pairs = n * rows
+    length = n // 2
     half = width // 2
     bf16, f32 = jnp.bfloat16, jnp.float32
     hbm = pl.BlockSpec(memory_space=pltpu.HBM)
@@ -399,23 +498,32 @@
             pltpu.VMEM((rows, width), bf16),
             pltpu.VMEM((depth, width), f32),
             pltpu.VMEM((n * depth, width), bf16),
-            pltpu.VMEM((pairs, width), bf16),
-            pltpu.VMEM((pairs, width), bf16),
+            pltpu.VMEM((length * rows, width), bf16),
+            pltpu.VMEM((2 * rows, width), bf16),
             pltpu.VMEM((n, rows, depth), bf16),
             pltpu.VMEM((n, depth, rows), bf16),
             pltpu.VMEM((rows, feat), bf16),
             pltpu.VMEM((rows, width), bf16),
-            pltpu.VMEM((n, rows, rows), f32),
-            pltpu.VMEM((n, 1, pairs + rows), f32),
-            pltpu.VMEM((1, pairs), f32),
+            pltpu.VMEM((2 * rows, length * rows), bf16),
+            pltpu.VMEM((2, 1, 2 * rows), f32),
+            pltpu.VMEM((length, 1, length * rows), f32),
+            pltpu.VMEM((rows, width), bf16),
+            pltpu.VMEM((rows, width), bf16),
+            pltpu.VMEM((length, rows, width), f32),
+            pltpu.VMEM((2, length - 1, rows, width), bf16),
+            pltpu.VMEM((2, length - 1, rows, width), bf16),
             pltpu.VMEM((2, n - 1, depth, half), bf16),
             pltpu.VMEM((2, n - 1, depth, half), bf16),
             pltpu.SemaphoreType.DMA((3,)),
             pltpu.SemaphoreType.DMA((3,)),
-            pltpu.SemaphoreType.DMA((4, 2, n - 1)),
-            pltpu.SemaphoreType.DMA((4, 2, n - 1)),
-            pltpu.SemaphoreType.DMA((n - 1,)),
-            pltpu.SemaphoreType.DMA((n - 1,)),
+            pltpu.SemaphoreType.DMA((2, 2, n - 1)),
+            pltpu.SemaphoreType.DMA((2, 2, n - 1)),
+            pltpu.SemaphoreType.DMA((3,)),
+            pltpu.SemaphoreType.DMA((3,)),
+            pltpu.SemaphoreType.DMA((length - 1,)),
+            pltpu.SemaphoreType.DMA((length - 1,)),
+            pltpu.SemaphoreType.DMA((2, 2, length - 1)),
+            pltpu.SemaphoreType.DMA((2, 2, length - 1)),
         ],
         compiler_params=pltpu.CompilerParams(
             collective_id=0, has_side_effects=True, vmem_limit_bytes=62 * 2**20
@@ -426,7 +534,12 @@
         out_shape=out_shape,
         in_specs=[hbm, hbm, hbm],
         out_specs=(hbm, hbm, hbm),
-        scratch_shapes=[pltpu.SemaphoreType.DMA((3,))],
+        scratch_shapes=[
+            pltpu.VMEM((rows, feat), bf16),
+            pltpu.VMEM((rows, width), bf16),
+            pltpu.VMEM((depth, width), f32),
+            pltpu.SemaphoreType.DMA((2, 3)),
+        ],
         compiler_params=pltpu.CompilerParams(vmem_limit_bytes=62 * 2**20),
     )(*results)
 

time: 89.7 us -> 65.6 us (0.73)
  Pallas kernels: 88.3 us -> 64.1 us
    pallas_call x1, Pallas kernels: 26.9 us -> 1.94 us  [local_kernel(): pl.pallas_call(hand_on_kernel, out_shape=out_shape, in_specs=[hbm, hbm, h...]
where the time goes in v4:
time: 65.6 us; the launch traced here: 65.4 us
  Pallas kernels  64.1 us (98%)
  between operations  1.29 us (2%)
    pallas_call x1, Pallas kernels, local_kernel(): pl.pallas_call(functools.partial(step_kernel, n), out_shape=out_shape, in...  62.2 us
    pallas_call x1, Pallas kernels, local_kernel(): pl.pallas_call(hand_on_kernel, out_shape=out_shape, in_specs=[hbm, hbm, h...  1.94 us

profile of v4, /device:TPU:0, one launch (start us, length us, event | category | flops | bytes accessed | tf_op | source)
XLA Modules:
  0.0 65.4 jit_solution(13933006399939670217)
XLA Ops:
  1.3 62.2 %shard_map.67 = (bf16[128,1408]{1,0:T(8,128)(2,1)}, bf16[128,512]{1,0:T(8,128)(2,1)}, f32[176,512]{1,0:T(8,128)}) custom-call(bf16[128,1408]{1,0:T(8,128)(2,1)} %feat_hbm.1, bf16[128,512]{1,0:T(8,128)(2,1)} %text_hbm.1, bf16[176,512]{1,0:T(8,128)(2,1)} %head_hbm.1, f32[1]{0:T(128)S(6)} %copy.7.scale_ref), custom_call_target="tpu_custom_call" | custom-call | tf_op jit(solution)/shard_map/pallas_call | solution.py:491
  63.5 1.9 %shard_map.68 = (bf16[128,1408]{1,0:T(8,128)(2,1)}, bf16[128,512]{1,0:T(8,128)(2,1)}, f32[176,512]{1,0:T(8,128)}) custom-call(bf16[128,1408]{1,0:T(8,128)(2,1)} %get-tuple-element.6.refs_0_, bf16[128,512]{1,0:T(8,128)(2,1)} %get-tuple-element.7.refs_1_, f32[176,512]{1,0:T(8,128)} %get-tuple-element.8.refs_2_), custom_call_target="tpu_custom_call" | custom-call | tf_op jit(solution)/shard_map/pallas_call | solution.py:532

commit v5 on v4

--- a/solution.py
+++ b/solution.py
@@ -154,11 +154,15 @@
     other = me + 1 - 2 * side
     partner = {+1: index_at(place + 1, n), -1: index_at(place - 1, n)}
 
-    own_head = head_all.at[pl.ds(pl.multiple_of(me * depth, 16), depth), :]
+    own_head = pl.ds(pl.multiple_of(me * depth, 16), depth)
     loads = [
-        pltpu.make_async_copy(head_hbm, own_head, load_sem.at[0]),
-        pltpu.make_async_copy(text_hbm, text_ref, load_sem.at[1]),
-        pltpu.make_async_copy(feat_hbm, feat_ref, load_sem.at[2]),
+        pltpu.make_async_copy(
+            head_hbm.at[:, pl.ds(c * half, half)], head_all.at[c, own_head, :], load_sem.at[2 + c]
+        )
+        for c in range(2)
+    ] + [
+        pltpu.make_async_copy(text_hbm, text_ref, load_sem.at[0]),
+        pltpu.make_async_copy(feat_hbm, feat_ref, load_sem.at[1]),
     ]
     stores = [
         pltpu.make_async_copy(feat_grad_ref, feat_out, store_sem.at[0]),
@@ -173,6 +177,7 @@
             barrier, inc=1, device_id={"dp": lax.rem(me + k, n)}, device_id_type=MESH
         )
     loads[0].wait()
+    loads[1].wait()
     pl.semaphore_wait(barrier, n - 1)
 
     def columns(way, m):
@@ -195,7 +200,8 @@
     def gather_copy(kind, way, m, origin_shift):
         buf, block = gathered[kind]
         owner = index_at(place - way * origin_shift, n)
-        ref = buf.at[pl.ds(pl.multiple_of(owner * block, 16), block), columns(way, m)]
+        at = pl.ds(pl.multiple_of(owner * block, 16), block)
+        ref = buf.at[columns(way, m).start // half, at, :]
         return remote(kind, way, m, ref, ref)
 
     def gather_send(kind, m):
@@ -262,36 +268,49 @@
     gather_send(HEAD, 0)
     gather_send(HEAD, 1)
 
-    loads[1].wait()
+    loads[2].wait()
     txt_emb = text_ref[...].astype(jnp.float32)
     txt_scaled, txt_inv = unit_rows(txt_emb)
     text_col[pl.ds(pl.multiple_of(level * rows, 16), rows), :] = txt_scaled.astype(jnp.bfloat16)
-    loads[2].wait()
+    gather_send(HEAD, 2)
+    loads[3].wait()
     feat_t = feat_ref[...].astype(jnp.float32).T
-    for b in range(n):
-        block = feat_t[b * depth : (b + 1) * depth]
-        feat_t_blocks[b] = block.astype(jnp.bfloat16)
-        feat_blocks[b] = block.T.astype(jnp.bfloat16)
+
+    def split_feat(first, last):
+        for b in range(first, last):
+            block = feat_t[b * depth : (b + 1) * depth]
+            feat_t_blocks[b] = block.astype(jnp.bfloat16)
+            feat_blocks[b] = block.T.astype(jnp.bfloat16)
+
+    split_feat(0, n // 2)
+    gather_send(HEAD, 3)
+    split_feat(n // 2, n)
 
     def emb_part(owner):
-        return jnp.dot(
-            feat_blocks[owner],
-            head_all[pl.ds(pl.multiple_of(owner * depth, 16), depth), :],
-            preferred_element_type=jnp.float32,
-        )
-
-    img_emb = emb_part(me)
-    for m in range(2, messages):
+        at = pl.ds(pl.multiple_of(owner * depth, 16), depth)
+        block = feat_blocks[owner]
+        return jnp.concatenate(
+            [
+                jnp.dot(block, head_all[c, at, :], preferred_element_type=jnp.float32)
+                for c in range(2)
+            ],
+            axis=1,
+        )
+
+    def emb_parts(shift):
+        return emb_part(index_at(place - shift, n)) + emb_part(index_at(place + shift, n))
+
+    gather_send(HEAD, 4)
+    img_emb = emb_part(me) + emb_parts(1)
+    for m in range(5, messages):
         gather_send(HEAD, m)
         if m % 2 == 1:
-            for way in (1, -1):
-                img_emb += emb_part(index_at(place - way * (m // 2), n))
+            img_emb += emb_parts(m // 2)
         if m == messages - 2:
             text_slot(0)
     gather_last(HEAD)
     text_slot(1)
-    for way in (1, -1):
-        img_emb += emb_part(index_at(place - way * (n // 2 - 1), n))
+    img_emb += emb_parts(n // 2 - 1)
     img_emb += emb_part(index_at(place + n // 2, n))
     img_scaled, img_inv = unit_rows(img_emb)
     img_unit = img_scaled.astype(jnp.bfloat16)
@@ -301,8 +320,12 @@
         text_slot(slot)
 
     scale = scale_ref[0]
+    own_exp = jnp.exp(tile_logits(scale, img_unit, text_col[...]))
     images_landed.wait_recv()
-    exp_tile = jnp.exp(tile_logits(scale, images[...], text_col[...]))
+    other_exp = jnp.exp(tile_logits(scale, images[other_images, :], text_col[...]))
+    exp_tile = jnp.concatenate(
+        [jnp.where(side == 0, own_exp, other_exp), jnp.where(side == 0, other_exp, own_exp)], axis=0
+    )
     row_part = jnp.sum(exp_tile, axis=1, keepdims=True)
     row_stats[side] = jnp.broadcast_to(row_part, (2 * rows, rows)).T[0:1, :]
     col_stats[level] = jnp.sum(exp_tile, axis=0, keepdims=True)
@@ -414,8 +437,14 @@
         stores[1].start()
 
     def feat_side():
-        feat_grad_ref[...] = lax.dot_general(
-            img_emb_grad, head_all[...], ROWS_ROWS, preferred_element_type=jnp.float32
+        feat_grad_ref[...] = sum(
+            lax.dot_general(
+                img_emb_grad[:, c * half : (c + 1) * half],
+                head_all[c],
+                ROWS_ROWS,
+                preferred_element_type=jnp.float32,
+            )
+            for c in range(2)
         ).astype(jnp.bfloat16)
         stores[0].start()
 
@@ -423,10 +452,8 @@
         grad_send(m)
         if m >= 1 and m <= length - 2:
             text_grad_slot(m)
-        if m == length - 1:
-            feat_side()
-        if m == messages - 2:
-            text_side()
+    feat_side()
+    text_side()
 
     total = [head_part(me, pl.ds(0, half)), head_part(me, pl.ds(half, half))]
     for m in range(messages - 2, messages):
@@ -497,7 +524,7 @@
             pltpu.VMEM((rows, feat), bf16),
             pltpu.VMEM((rows, width), bf16),
             pltpu.VMEM((depth, width), f32),
-            pltpu.VMEM((n * depth, width), bf16),
+            pltpu.VMEM((2, n * depth, half), bf16),
             pltpu.VMEM((length * rows, width), bf16),
             pltpu.VMEM((2 * rows, width), bf16),
             pltpu.VMEM((n, rows, depth), bf16),
@@ -514,7 +541,7 @@
             pltpu.VMEM((2, length - 1, rows, width), bf16),
             pltpu.VMEM((2, n - 1, depth, half), bf16),
             pltpu.VMEM((2, n - 1, depth, half), bf16),
-            pltpu.SemaphoreType.DMA((3,)),
+            pltpu.SemaphoreType.DMA((4,)),
             pltpu.SemaphoreType.DMA((3,)),
             pltpu.SemaphoreType.DMA((2, 2, n - 1)),
             pltpu.SemaphoreType.DMA((2, 2, n - 1)),
@@ -549,7 +576,7 @@
     size = 24 * pairs * rows + 4 * pairs * width + 8 * n * depth * width + 12 * rows * feat
     return (
         n % 2 == 0
-        and n >= 6
+        and n >= 8
         and rows % 128 == 0
         and width % 256 == 0
         and depth % 16 == 0

time: 65.6 us -> 65.9 us (level)
  no operation moved by 1% of the time
where the time goes in v5:
time: 65.9 us; the launch traced here: 65.7 us
  Pallas kernels  64.5 us (98%)
  between operations  1.29 us (2%)
    pallas_call x1, Pallas kernels, local_kernel(): pl.pallas_call(functools.partial(step_kernel, n), out_shape=out_shape, in...  62.5 us
    pallas_call x1, Pallas kernels, local_kernel(): pl.pallas_call(hand_on_kernel, out_shape=out_shape, in_specs=[hbm, hbm, h...  1.94 us

profile of v5, /device:TPU:0, one launch (start us, length us, event | category | flops | bytes accessed | tf_op | source)
XLA Modules:
  0.0 65.7 jit_solution(13507129843010345813)
XLA Ops:
  1.3 62.5 %shard_map.67 = (bf16[128,1408]{1,0:T(8,128)(2,1)}, bf16[128,512]{1,0:T(8,128)(2,1)}, f32[176,512]{1,0:T(8,128)}) custom-call(bf16[128,1408]{1,0:T(8,128)(2,1)} %feat_hbm.1, bf16[128,512]{1,0:T(8,128)(2,1)} %text_hbm.1, bf16[176,512]{1,0:T(8,128)(2,1)} %head_hbm.1, f32[1]{0:T(128)S(6)} %copy.7.scale_ref), custom_call_target="tpu_custom_call" | custom-call | tf_op jit(solution)/shard_map/pallas_call | solution.py:518
  63.8 1.9 %shard_map.68 = (bf16[128,1408]{1,0:T(8,128)(2,1)}, bf16[128,512]{1,0:T(8,128)(2,1)}, f32[176,512]{1,0:T(8,128)}) custom-call(bf16[128,1408]{1,0:T(8,128)(2,1)} %get-tuple-element.6.refs_0_, bf16[128,512]{1,0:T(8,128)(2,1)} %get-tuple-element.7.refs_1_, f32[176,512]{1,0:T(8,128)} %get-tuple-element.8.refs_2_), custom_call_target="tpu_custom_call" | custom-call | tf_op jit(solution)/shard_map/pallas_call | solution.py:559

commit v6 on v4

--- a/solution.py
+++ b/solution.py
@@ -86,6 +86,7 @@
 
 
 MESH = pl.DeviceIdType.MESH
+CHUNKS = 4
 HEAD, GRAD = range(2)
 IMAGES, IMAGE_GRADS, ROW_SUMS = range(3)
 ROWS_ROWS = (((1,), (1,)), ((), ()))
@@ -145,20 +146,20 @@
 ):
     rows, width = text_hbm.shape
     depth = head_hbm.shape[0]
-    half = width // 2
+    chunk = width // CHUNKS
     length = n // 2
-    messages = n - 1
+    messages = CHUNKS * (n - 1) // 2
     me = lax.axis_index("dp")
     place = place_of(me, n)
     level, side = lax.div(me, 2), lax.rem(me, 2)
     other = me + 1 - 2 * side
     partner = {+1: index_at(place + 1, n), -1: index_at(place - 1, n)}
 
-    own_head = head_all.at[pl.ds(pl.multiple_of(me * depth, 16), depth), :]
+    own_head = pl.ds(pl.multiple_of(me * depth, 16), depth)
     loads = [
-        pltpu.make_async_copy(head_hbm, own_head, load_sem.at[0]),
-        pltpu.make_async_copy(text_hbm, text_ref, load_sem.at[1]),
-        pltpu.make_async_copy(feat_hbm, feat_ref, load_sem.at[2]),
+        pltpu.make_async_copy(head_hbm, head_all.at[own_head, :], load_sem.at[2]),
+        pltpu.make_async_copy(text_hbm, text_ref, load_sem.at[0]),
+        pltpu.make_async_copy(feat_hbm, feat_ref, load_sem.at[1]),
     ]
     stores = [
         pltpu.make_async_copy(feat_grad_ref, feat_out, store_sem.at[0]),
@@ -176,8 +177,7 @@
     pl.semaphore_wait(barrier, n - 1)
 
     def columns(way, m):
-        first = (m % 2 == 0) == (way == 1)
-        return pl.ds(0 if first else half, half)
+        return pl.ds((m % CHUNKS + (0 if way == 1 else CHUNKS // 2)) % CHUNKS * chunk, chunk)
 
     def remote(kind, way, m, src, dst):
         side = 0 if way == 1 else 1
@@ -195,19 +195,21 @@
     def gather_copy(kind, way, m, origin_shift):
         buf, block = gathered[kind]
         owner = index_at(place - way * origin_shift, n)
-        ref = buf.at[pl.ds(pl.multiple_of(owner * block, 16), block), columns(way, m)]
+        at = pl.ds(pl.multiple_of(owner * block, 16), block)
+        ref = buf.at[at, columns(way, m)]
         return remote(kind, way, m, ref, ref)
 
-    def gather_send(kind, m):
-        for way in (1, -1):
-            if m >= 2:
-                gather_copy(kind, way, m - 2, m // 2).wait_recv()
-            gather_copy(kind, way, m, m // 2).start()
+    def gather_send(kind, step):
+        for m in range(step * CHUNKS, min((step + 1) * CHUNKS, messages)):
+            for way in (1, -1):
+                if step >= 1:
+                    gather_copy(kind, way, m - CHUNKS, step).wait_recv()
+                gather_copy(kind, way, m, step).start()
 
     def gather_last(kind):
-        for m in range(max(messages - 2, 0), messages):
+        for m in range(messages - CHUNKS, messages):
             for way in (1, -1):
-                gather_copy(kind, way, m, m // 2 + 1).wait_recv()
+                gather_copy(kind, way, m, m // CHUNKS + 1).wait_recv()
 
     def along(way):
         return level if way == 1 else length - 1 - level
@@ -260,12 +262,12 @@
     sums_landed = pair_copy(ROW_SUMS, row_stats.at[1 - side], row_stats.at[1 - side])
 
     gather_send(HEAD, 0)
-    gather_send(HEAD, 1)
 
     loads[1].wait()
     txt_emb = text_ref[...].astype(jnp.float32)
     txt_scaled, txt_inv = unit_rows(txt_emb)
     text_col[pl.ds(pl.multiple_of(level * rows, 16), rows), :] = txt_scaled.astype(jnp.bfloat16)
+    text_slot(0)
     loads[2].wait()
     feat_t = feat_ref[...].astype(jnp.float32).T
     for b in range(n):
@@ -274,35 +276,36 @@
         feat_blocks[b] = block.T.astype(jnp.bfloat16)
 
     def emb_part(owner):
-        return jnp.dot(
-            feat_blocks[owner],
-            head_all[pl.ds(pl.multiple_of(owner * depth, 16), depth), :],
-            preferred_element_type=jnp.float32,
-        )
-
-    img_emb = emb_part(me)
-    for m in range(2, messages):
-        gather_send(HEAD, m)
-        if m % 2 == 1:
-            for way in (1, -1):
-                img_emb += emb_part(index_at(place - way * (m // 2), n))
-        if m == messages - 2:
-            text_slot(0)
+        at = pl.ds(pl.multiple_of(owner * depth, 16), depth)
+        block = feat_blocks[owner]
+        return jnp.dot(block, head_all[at, :], preferred_element_type=jnp.float32)
+
+    def emb_parts(shift):
+        return emb_part(index_at(place - shift, n)) + emb_part(index_at(place + shift, n))
+
+    img_emb = None
+    for step in range(1, length):
+        gather_send(HEAD, step)
+        if step < length - 1:
+            text_slot(step)
+        part = emb_parts(step - 1) if step > 1 else emb_part(me)
+        img_emb = part if img_emb is None else img_emb + part
     gather_last(HEAD)
-    text_slot(1)
-    for way in (1, -1):
-        img_emb += emb_part(index_at(place - way * (n // 2 - 1), n))
-    img_emb += emb_part(index_at(place + n // 2, n))
+    img_emb += emb_parts(length - 1)
+    img_emb += emb_part(index_at(place + length, n))
     img_scaled, img_inv = unit_rows(img_emb)
     img_unit = img_scaled.astype(jnp.bfloat16)
     images[own_images, :] = img_unit
     images_copy.start()
-    for slot in range(2, length):
-        text_slot(slot)
+    text_slot(length - 1)
 
     scale = scale_ref[0]
+    own_exp = jnp.exp(tile_logits(scale, img_unit, text_col[...]))
     images_landed.wait_recv()
-    exp_tile = jnp.exp(tile_logits(scale, images[...], text_col[...]))
+    other_exp = jnp.exp(tile_logits(scale, images[other_images, :], text_col[...]))
+    exp_tile = jnp.concatenate(
+        [jnp.where(side == 0, own_exp, other_exp), jnp.where(side == 0, other_exp, own_exp)], axis=0
+    )
     row_part = jnp.sum(exp_tile, axis=1, keepdims=True)
     row_stats[side] = jnp.broadcast_to(row_part, (2 * rows, rows)).T[0:1, :]
     col_stats[level] = jnp.sum(exp_tile, axis=0, keepdims=True)
@@ -383,7 +386,7 @@
     def head_part(owner, cols):
         return jnp.dot(
             feat_t_blocks[owner],
-            img_emb_grad[:, cols.start : cols.start + half],
+            img_emb_grad[:, cols.start : cols.start + cols.size],
             preferred_element_type=jnp.float32,
         )
 
@@ -391,15 +394,17 @@
         side = 0 if way == 1 else 1
         return remote(GRAD, way, m, outgoing.at[side, m], incoming.at[side, m])
 
-    def grad_send(m):
-        for way in (1, -1):
-            side = 0 if way == 1 else 1
-            value = head_part(index_at(place + way * (n // 2 - (m + 1) // 2), n), columns(way, m))
-            if m >= 2:
-                grad_copy(way, m - 2).wait_recv()
-                value += incoming[side, m - 2].astype(jnp.float32)
-            outgoing[side, m] = value.astype(jnp.bfloat16)
-            grad_copy(way, m).start()
+    def grad_send(step):
+        for m in range(step * CHUNKS, min((step + 1) * CHUNKS, messages)):
+            far = length - step - (0 if m % CHUNKS < CHUNKS // 2 else 1)
+            for way in (1, -1):
+                side = 0 if way == 1 else 1
+                value = head_part(index_at(place + way * far, n), columns(way, m))
+                if step >= 1:
+                    grad_copy(way, m - CHUNKS).wait_recv()
+                    value += incoming[side, m - CHUNKS].astype(jnp.float32)
+                outgoing[side, m] = value.astype(jnp.bfloat16)
+                grad_copy(way, m).start()
 
     def text_side():
         for way in (1, -1):
@@ -419,23 +424,23 @@
         ).astype(jnp.bfloat16)
         stores[0].start()
 
-    for m in range(messages):
-        grad_send(m)
-        if m >= 1 and m <= length - 2:
-            text_grad_slot(m)
-        if m == length - 1:
-            feat_side()
-        if m == messages - 2:
-            text_side()
-
-    total = [head_part(me, pl.ds(0, half)), head_part(me, pl.ds(half, half))]
-    for m in range(messages - 2, messages):
+    for step in range(length):
+        grad_send(step)
+        if 1 <= step <= length - 2:
+            text_grad_slot(step)
+    feat_side()
+    text_side()
+
+    total = head_part(me, pl.ds(0, width))
+    arrived = {0: [None] * CHUNKS, 1: [None] * CHUNKS}
+    for m in range(messages - CHUNKS, messages):
         for way in (1, -1):
             grad_copy(way, m).wait_recv()
-            which = columns(way, m).start // half
-            total[which] += incoming[0 if way == 1 else 1, m].astype(jnp.float32)
-    head_grad_ref[:, 0:half] = total[0]
-    head_grad_ref[:, half:width] = total[1]
+            which = 0 if way == 1 else 1
+            arrived[which][columns(way, m).start // chunk] = incoming[which, m].astype(jnp.float32)
+    head_grad_ref[...] = (
+        total + jnp.concatenate(arrived[0], axis=1) + jnp.concatenate(arrived[1], axis=1)
+    )
     stores[2].start()
 
     for m in range(messages):
@@ -480,7 +485,8 @@
     rows, width = text_embed.shape
     depth, feat = image_head.shape[0], image_features.shape[1]
     length = n // 2
-    half = width // 2
+    chunk = width // CHUNKS
+    messages = CHUNKS * (n - 1) // 2
     bf16, f32 = jnp.bfloat16, jnp.float32
     hbm = pl.BlockSpec(memory_space=pltpu.HBM)
     out_shape = (
@@ -512,12 +518,12 @@
             pltpu.VMEM((length, rows, width), f32),
             pltpu.VMEM((2, length - 1, rows, width), bf16),
             pltpu.VMEM((2, length - 1, rows, width), bf16),
-            pltpu.VMEM((2, n - 1, depth, half), bf16),
-            pltpu.VMEM((2, n - 1, depth, half), bf16),
+            pltpu.VMEM((2, messages, depth, chunk), bf16),
+            pltpu.VMEM((2, messages, depth, chunk), bf16),
             pltpu.SemaphoreType.DMA((3,)),
             pltpu.SemaphoreType.DMA((3,)),
-            pltpu.SemaphoreType.DMA((2, 2, n - 1)),
-            pltpu.SemaphoreType.DMA((2, 2, n - 1)),
+            pltpu.SemaphoreType.DMA((2, 2, messages)),
+            pltpu.SemaphoreType.DMA((2, 2, messages)),
             pltpu.SemaphoreType.DMA((3,)),
             pltpu.SemaphoreType.DMA((3,)),
             pltpu.SemaphoreType.DMA((length - 1,)),
@@ -549,9 +555,9 @@
     size = 24 * pairs * rows + 4 * pairs * width + 8 * n * depth * width + 12 * rows * feat
     return (
         n % 2 == 0
-        and n >= 6
+        and n >= 8
         and rows % 128 == 0
-        and width % 256 == 0
+        and width % (128 * CHUNKS) == 0
         and depth % 16 == 0
         and feat == n * depth
         and size <= 24 * 2**20

time: 65.6 us -> 67.3 us (1.026)
  Pallas kernels: 64.1 us -> 65.8 us
    pallas_call x1, Pallas kernels: 62.2 us -> 63.9 us  [local_kernel(): pl.pallas_call(functools.partial(step_kernel, n), out_shape=out_shape, in...]
where the time goes in v6:
time: 67.3 us; the launch traced here: 67.1 us
  Pallas kernels  65.8 us (98%)
  between operations  1.29 us (2%)
    pallas_call x1, Pallas kernels, local_kernel(): pl.pallas_call(functools.partial(step_kernel, n), out_shape=out_shape, in...  63.9 us
    pallas_call x1, Pallas kernels, local_kernel(): pl.pallas_call(hand_on_kernel, out_shape=out_shape, in_specs=[hbm, hbm, h...  1.94 us

profile of v6, /device:TPU:0, one launch (start us, length us, event | category | flops | bytes accessed | tf_op | source)
XLA Modules:
  0.0 67.1 jit_solution(17129416896984082944)
XLA Ops:
  1.3 63.9 %shard_map.67 = (bf16[128,1408]{1,0:T(8,128)(2,1)}, bf16[128,512]{1,0:T(8,128)(2,1)}, f32[176,512]{1,0:T(8,128)}) custom-call(bf16[128,1408]{1,0:T(8,128)(2,1)} %feat_hbm.1, bf16[128,512]{1,0:T(8,128)(2,1)} %text_hbm.1, bf16[176,512]{1,0:T(8,128)(2,1)} %head_hbm.1, f32[1]{0:T(128)S(6)} %copy.7.scale_ref), custom_call_target="tpu_custom_call" | custom-call | tf_op jit(solution)/shard_map/pallas_call | solution.py:497
  65.1 1.9 %shard_map.68 = (bf16[128,1408]{1,0:T(8,128)(2,1)}, bf16[128,512]{1,0:T(8,128)(2,1)}, f32[176,512]{1,0:T(8,128)}) custom-call(bf16[128,1408]{1,0:T(8,128)(2,1)} %get-tuple-element.6.refs_0_, bf16[128,512]{1,0:T(8,128)(2,1)} %get-tuple-element.7.refs_1_, f32[176,512]{1,0:T(8,128)} %get-tuple-element.8.refs_2_), custom_call_target="tpu_custom_call" | custom-call | tf_op jit(solution)/shard_map/pallas_call | solution.py:538

commit v7 on v6

--- a/solution.py
+++ b/solution.py
@@ -86,7 +86,7 @@
 
 
 MESH = pl.DeviceIdType.MESH
-CHUNKS = 4
+CHUNKS = 2
 HEAD, GRAD = range(2)
 IMAGES, IMAGE_GRADS, ROW_SUMS = range(3)
 ROWS_ROWS = (((1,), (1,)), ((), ()))

time: 67.3 us -> 67.3 us (level)
  no operation moved by 1% of the time
where the time goes in v7:
time: 67.3 us; the launch traced here: 67.2 us
  Pallas kernels  65.9 us (98%)
  between operations  1.29 us (2%)
    pallas_call x1, Pallas kernels, local_kernel(): pl.pallas_call(functools.partial(step_kernel, n), out_shape=out_shape, in...  63.9 us
    pallas_call x1, Pallas kernels, local_kernel(): pl.pallas_call(hand_on_kernel, out_shape=out_shape, in_specs=[hbm, hbm, h...  1.94 us

profile of v7, /device:TPU:0, one launch (start us, length us, event | category | flops | bytes accessed | tf_op | source)
XLA Modules:
  0.0 67.2 jit_solution(10985311072948917994)
XLA Ops:
  1.3 63.9 %shard_map.67 = (bf16[128,1408]{1,0:T(8,128)(2,1)}, bf16[128,512]{1,0:T(8,128)(2,1)}, f32[176,512]{1,0:T(8,128)}) custom-call(bf16[128,1408]{1,0:T(8,128)(2,1)} %feat_hbm.1, bf16[128,512]{1,0:T(8,128)(2,1)} %text_hbm.1, bf16[176,512]{1,0:T(8,128)(2,1)} %head_hbm.1, f32[1]{0:T(128)S(6)} %copy.7.scale_ref), custom_call_target="tpu_custom_call" | custom-call | tf_op jit(solution)/shard_map/pallas_call | solution.py:497
  65.2 1.9 %shard_map.68 = (bf16[128,1408]{1,0:T(8,128)(2,1)}, bf16[128,512]{1,0:T(8,128)(2,1)}, f32[176,512]{1,0:T(8,128)}) custom-call(bf16[128,1408]{1,0:T(8,128)(2,1)} %get-tuple-element.6.refs_0_, bf16[128,512]{1,0:T(8,128)(2,1)} %get-tuple-element.7.refs_1_, f32[176,512]{1,0:T(8,128)} %get-tuple-element.8.refs_2_), custom_call_target="tpu_custom_call" | custom-call | tf_op jit(solution)/shard_map/pallas_call | solution.py:538

commit v8 on v3

--- a/solution.py
+++ b/solution.py
@@ -203,6 +203,7 @@
     txt_emb = text_ref[...].astype(jnp.float32)
     txt_scaled, txt_inv = unit_rows(txt_emb)
     text_all[pl.ds(pl.multiple_of(me * rows, 16), rows), :] = txt_scaled.astype(jnp.bfloat16)
+    gather_send(HEAD, 2)
     loads[2].wait()
     feat_t = feat_ref[...].astype(jnp.float32).T
     for b in range(n):
@@ -217,8 +218,11 @@
             preferred_element_type=jnp.float32,
         )
 
+    gather_send(HEAD, 3)
     img_emb = emb_part(me)
-    for m in range(2, messages):
+    for way in (1, -1):
+        img_emb += emb_part(index_at(place - way, n))
+    for m in range(4, messages):
         gather_send(HEAD, m)
         if m % 2 == 1:
             for way in (1, -1):
@@ -338,12 +342,10 @@
         if m >= 1 and image_sent < messages:
             gather_send(IMAGE, image_sent)
             image_sent += 1
-        if m == 2:
-            feat_side()
-        if m == messages - 2:
-            gather_last(IMAGE)
-            text_side()
-
+
+    feat_side()
+    gather_last(IMAGE)
+    text_side()
     total = [head_part(me, pl.ds(0, half)), head_part(me, pl.ds(half, half))]
     for m in range(messages - 2, messages):
         for way in (1, -1):
@@ -366,15 +368,16 @@
 
 
 def hand_on_kernel(*refs):
-    sources, results, sem = refs[:3], refs[3:6], refs[6]
-    copies = [
-        pltpu.make_async_copy(source, result, sem.at[i])
-        for i, (source, result) in enumerate(zip(sources, results))
-    ]
-    for copy in copies:
-        copy.start()
-    for copy in copies:
-        copy.wait()
+    sources, results, held, sem = refs[:3], refs[3:6], refs[6:9], refs[9]
+    loads = [pltpu.make_async_copy(sources[i], held[i], sem.at[0, i]) for i in range(3)]
+    stores = [pltpu.make_async_copy(held[i], results[i], sem.at[1, i]) for i in range(3)]
+    for load in loads:
+        load.start()
+    for load, store in zip(loads, stores):
+        load.wait()
+        store.start()
+    for store in stores:
+        store.wait()
 
 
 def local_kernel(n, image_features, text_embed, image_head, logit_scale):
@@ -426,7 +429,12 @@
         out_shape=out_shape,
         in_specs=[hbm, hbm, hbm],
         out_specs=(hbm, hbm, hbm),
-        scratch_shapes=[pltpu.SemaphoreType.DMA((3,))],
+        scratch_shapes=[
+            pltpu.VMEM((rows, feat), bf16),
+            pltpu.VMEM((rows, width), bf16),
+            pltpu.VMEM((depth, width), f32),
+            pltpu.SemaphoreType.DMA((2, 3)),
+        ],
         compiler_params=pltpu.CompilerParams(vmem_limit_bytes=62 * 2**20),
     )(*results)
 
@@ -436,7 +444,7 @@
     size = 24 * pairs * rows + 4 * pairs * width + 8 * n * depth * width + 12 * rows * feat
     return (
         n % 2 == 0
-        and n >= 6
+        and n >= 8
         and rows % 128 == 0
         and width % 256 == 0
         and depth % 16 == 0

time: 89.7 us -> 64.7 us (0.72)
  Pallas kernels: 88.3 us -> 63.3 us
    pallas_call x1, Pallas kernels: 26.9 us -> 1.94 us  [local_kernel(): pl.pallas_call(hand_on_kernel, out_shape=out_shape, in_specs=[hbm, hbm, h...]
where the time goes in v8:
time: 64.7 us; the launch traced here: 64.5 us
  Pallas kernels  63.3 us (98%)
  between operations  1.29 us (2%)
    pallas_call x1, Pallas kernels, local_kernel(): pl.pallas_call(functools.partial(step_kernel, n), out_shape=out_shape, in...  61.3 us
    pallas_call x1, Pallas kernels, local_kernel(): pl.pallas_call(hand_on_kernel, out_shape=out_shape, in_specs=[hbm, hbm, h...  1.94 us

profile of v8, /device:TPU:0, one launch (start us, length us, event | category | flops | bytes accessed | tf_op | source)
XLA Modules:
  0.0 64.5 jit_solution(3947126842468439357)
XLA Ops:
  1.3 61.3 %shard_map.67 = (bf16[128,1408]{1,0:T(8,128)(2,1)}, bf16[128,512]{1,0:T(8,128)(2,1)}, f32[176,512]{1,0:T(8,128)}) custom-call(bf16[128,1408]{1,0:T(8,128)(2,1)} %feat_hbm.1, bf16[128,512]{1,0:T(8,128)(2,1)} %text_hbm.1, bf16[176,512]{1,0:T(8,128)(2,1)} %head_hbm.1, f32[1]{0:T(128)S(6)} %copy.7.scale_ref), custom_call_target="tpu_custom_call" | custom-call | tf_op jit(solution)/shard_map/pallas_call | solution.py:395
  62.6 1.9 %shard_map.68 = (bf16[128,1408]{1,0:T(8,128)(2,1)}, bf16[128,512]{1,0:T(8,128)(2,1)}, f32[176,512]{1,0:T(8,128)}) custom-call(bf16[128,1408]{1,0:T(8,128)(2,1)} %get-tuple-element.6.refs_0_, bf16[128,512]{1,0:T(8,128)(2,1)} %get-tuple-element.7.refs_1_, f32[176,512]{1,0:T(8,128)} %get-tuple-element.8.refs_2_), custom_call_target="tpu_custom_call" | custom-call | tf_op jit(solution)/shard_map/pallas_call | solution.py:427

commit v9 on v8

--- a/solution.py
+++ b/solution.py
@@ -369,8 +369,18 @@
 
 def hand_on_kernel(*refs):
     sources, results, held, sem = refs[:3], refs[3:6], refs[6:9], refs[9]
-    loads = [pltpu.make_async_copy(sources[i], held[i], sem.at[0, i]) for i in range(3)]
-    stores = [pltpu.make_async_copy(held[i], results[i], sem.at[1, i]) for i in range(3)]
+    loads, stores = [], []
+    for part in range(2):
+        for i in range(3):
+            size = held[i].shape[0] // 2
+            at = pl.ds(part * size, size)
+            k = 3 * part + i
+            loads.append(
+                pltpu.make_async_copy(sources[i].at[at, :], held[i].at[at, :], sem.at[0, k])
+            )
+            stores.append(
+                pltpu.make_async_copy(held[i].at[at, :], results[i].at[at, :], sem.at[1, k])
+            )
     for load in loads:
         load.start()
     for load, store in zip(loads, stores):
@@ -433,7 +443,7 @@
             pltpu.VMEM((rows, feat), bf16),
             pltpu.VMEM((rows, width), bf16),
             pltpu.VMEM((depth, width), f32),
-            pltpu.SemaphoreType.DMA((2, 3)),
+            pltpu.SemaphoreType.DMA((2, 6)),
         ],
         compiler_params=pltpu.CompilerParams(vmem_limit_bytes=62 * 2**20),
     )(*results)

time: 64.7 us -> 64.8 us (level)
  no operation moved by 1% of the time
where the time goes in v9:
time: 64.8 us; the launch traced here: 64.6 us
  Pallas kernels  63.3 us (98%)
  between operations  1.29 us (2%)
    pallas_call x1, Pallas kernels, local_kernel(): pl.pallas_call(functools.partial(step_kernel, n), out_shape=out_shape, in...  61.3 us
    pallas_call x1, Pallas kernels, local_kernel(): pl.pallas_call(hand_on_kernel, out_shape=out_shape, in_specs=[hbm, hbm, h...  2.02 us

profile of v9, /device:TPU:0, one launch (start us, length us, event | category | flops | bytes accessed | tf_op | source)
XLA Modules:
  0.0 64.6 jit_solution(2932298204529426937)
XLA Ops:
  1.3 61.3 %shard_map.67 = (bf16[128,1408]{1,0:T(8,128)(2,1)}, bf16[128,512]{1,0:T(8,128)(2,1)}, f32[176,512]{1,0:T(8,128)}) custom-call(bf16[128,1408]{1,0:T(8,128)(2,1)} %feat_hbm.1, bf16[128,512]{1,0:T(8,128)(2,1)} %text_hbm.1, bf16[176,512]{1,0:T(8,128)(2,1)} %head_hbm.1, f32[1]{0:T(128)S(6)} %copy.7.scale_ref), custom_call_target="tpu_custom_call" | custom-call | tf_op jit(solution)/shard_map/pallas_call | solution.py:405
  62.6 2.0 %shard_map.68 = (bf16[128,1408]{1,0:T(8,128)(2,1)}, bf16[128,512]{1,0:T(8,128)(2,1)}, f32[176,512]{1,0:T(8,128)}) custom-call(bf16[128,1408]{1,0:T(8,128)(2,1)} %get-tuple-element.6.refs_0_, bf16[128,512]{1,0:T(8,128)(2,1)} %get-tuple-element.7.refs_1_, f32[176,512]{1,0:T(8,128)} %get-tuple-element.8.refs_2_), custom_call_target="tpu_custom_call" | custom-call | tf_op jit(solution)/shard_map/pallas_call | solution.py:437
